TPU v7x, 256 devices: a whole 4x4x8 slice. The times are simulated.
256 devices in a mesh: ctx: 16 (over y, x), sub: 16 (over z, core).
Axes of the slice: x: 4, y: 4, z: 8, core: 2. Of those that a mesh axis runs over, the one named last changes fastest.
Arguments:
- stream: bfloat16 [65536, 1536], P(('ctx', 'sub')), may hold values from -18 to 18
- query_full: bfloat16 [65536, 1536], P(('ctx', 'sub')), may hold values from -122 to 122
- key_full: bfloat16 [65536, 1536], P(('ctx', 'sub')), may hold values from -6 to 6
- value_full: bfloat16 [65536, 1536], P(('ctx', 'sub')), may hold values from -6 to 6
- pool_fine: float32 [4, 1536], replicated, may hold values from -3 to 3
- pool_coarse: float32 [4, 1536], replicated, may hold values from -3 to 3
- up_fine: float32 [4, 1536], replicated, may hold values from -4 to 4
- up_coarse: float32 [4, 1536], replicated, may hold values from -4 to 4
- norm_gain: float32 [1536], replicated, may hold values from 0.1 to 1.9
- coarse_qkv: bfloat16 [1536, 2304], P(None, 'sub'), may hold values from -8 to 8
- coarse_out: bfloat16 [768, 1536], P(None, 'sub'), may hold values from -0.21875 to 0.21875
Outputs:
- restored: bfloat16 [65536, 1536], P(('ctx', 'sub'))
All inputs are finite; a program needn't handle non-finite values.
Results may differ from a plain program's by a relative error of at most 0.0052.
The roundings to bfloat16 on the way count: a program that leaves them out, or rounds other values in their place, can miss the bound.
Values may be sent and summed in bfloat16 or wider, within the bound.
A program may use at most 128 MiB of HBM per device.

v0:
```python
import math

import jax
import jax.numpy as jnp
from jax import lax
from jax.sharding import PartitionSpec as P

HEADS = 12
HEAD_DIM = 128
SHORT = 4
WIN = 1536


NEGATIVE = -1e30


def shifted(value, axis, by):
    count = lax.axis_size(axis)
    pairs = [(i, i + by) for i in range(count) if 0 <= i + by < count]
    return lax.ppermute(value, axis, pairs)


def combine_rows(row_block, weights):
    row_count = row_block.shape[0] // SHORT
    grouped = row_block.astype(jnp.float32).reshape(row_count, SHORT, row_block.shape[1])
    return jnp.sum(grouped * weights[None, :, :], axis=1).astype(jnp.bfloat16)


def empty_state(head_count, row_count):
    return (
        jnp.full((head_count, row_count), NEGATIVE, jnp.float32),
        jnp.zeros((head_count, row_count), jnp.float32),
        jnp.zeros((head_count, row_count, HEAD_DIM), jnp.float32),
    )


def fold_block(state_carry, head_queries, key_rows, value_rows, allowed_mask):
    peak_before, total_before, summed_before = state_carry
    head_count = head_queries.shape[0]
    row_count = key_rows.shape[0]
    key_heads = key_rows.reshape(row_count, head_count, HEAD_DIM)
    value_heads = value_rows.reshape(row_count, head_count, HEAD_DIM)
    scores = jnp.einsum(
        "hqd,khd->hqk", head_queries, key_heads, preferred_element_type=jnp.float32
    ) * (1.0 / math.sqrt(HEAD_DIM))
    scores = jnp.where(allowed_mask[None], scores, NEGATIVE)
    peak_score = jnp.maximum(peak_before, jnp.max(scores, axis=2))
    weights = jnp.where(allowed_mask[None], jnp.exp(scores - peak_score[:, :, None]), 0.0)
    total_sum = jnp.sum(weights, axis=2)
    summed = jnp.einsum(
        "hqk,khd->hqd",
        weights.astype(jnp.bfloat16),
        value_heads,
        preferred_element_type=jnp.float32,
    )
    return (peak_score, total_sum, summed)


def finish_heads(state_carry):
    summed = state_carry[2] / state_carry[1][:, :, None]
    head_count, row_count, head_width = summed.shape
    return (
        summed.transpose(1, 0, 2).reshape(row_count, head_count * head_width).astype(jnp.bfloat16)
    )


def make_heads(allowed_mask, score_scale):

    def head_output(operands):
        query_one, key_one, value_one = operands
        scores = jnp.dot(query_one, key_one.T, preferred_element_type=jnp.float32) * score_scale
        scores = jnp.where(allowed_mask, scores, NEGATIVE)
        peak_score = jnp.max(scores, axis=1, keepdims=True)
        weights = jnp.where(allowed_mask, jnp.exp(scores - peak_score), 0.0)
        total_sum = jnp.sum(weights, axis=1, keepdims=True)
        return (
            jnp.dot(weights.astype(jnp.bfloat16), value_one, preferred_element_type=jnp.float32)
            / total_sum
        )

    return head_output


def shards(
    stream,
    query_full,
    key_full,
    value_full,
    pool_fine,
    pool_coarse,
    up_fine,
    up_coarse,
    norm_gain,
    coarse_qkv,
    coarse_out,
):
    local_rows = stream.shape[0]
    width = stream.shape[1]
    sub_count = lax.axis_size("sub")
    device = lax.axis_index("ctx") * sub_count + lax.axis_index("sub")
    score_scale = 1.0 / math.sqrt(HEAD_DIM)
    reach = WIN // local_rows
    key_value = jnp.stack([key_full, value_full])
    window_parts = [key_value]
    for offset_back in range(1, reach + 1):
        window_parts.insert(0, shifted(key_value, ("ctx", "sub"), offset_back))
    window = jnp.concatenate(window_parts, axis=1)
    key_span = window.shape[1]
    query_pos = device * local_rows + jnp.arange(local_rows, dtype=jnp.int32)
    key_pos = (device - reach) * local_rows + jnp.arange(key_span, dtype=jnp.int32)
    allowed_mask = (
        (key_pos[None, :] <= query_pos[:, None])
        & (key_pos[None, :] > query_pos[:, None] - WIN)
        & (key_pos[None, :] >= 0)
    )
    query_heads = query_full.reshape(local_rows, HEADS, HEAD_DIM).transpose(1, 0, 2)
    key_heads = window[0].reshape(key_span, HEADS, HEAD_DIM).transpose(1, 0, 2)
    value_heads = window[1].reshape(key_span, HEADS, HEAD_DIM).transpose(1, 0, 2)
    attended_fine = lax.map(
        make_heads(allowed_mask, score_scale), (query_heads, key_heads, value_heads)
    )
    attended_fine = attended_fine.transpose(1, 0, 2).reshape(local_rows, width)
    fine_stream = (stream.astype(jnp.float32) + attended_fine).astype(jnp.bfloat16)
    rim_count = SHORT - 1
    edge_rows = shifted(fine_stream[local_rows - rim_count :], ("ctx", "sub"), 1)
    middle_rows = combine_rows(
        jnp.concatenate([edge_rows, fine_stream], axis=0)[:local_rows], pool_fine
    )
    middle_count = middle_rows.shape[0]
    middle_edge = shifted(middle_rows[middle_count - rim_count :], ("ctx", "sub"), 1)
    summit_rows = combine_rows(
        jnp.concatenate([middle_edge, middle_rows], axis=0)[:middle_count], pool_coarse
    )
    top_count = summit_rows.shape[0]
    summit_wide = summit_rows.astype(jnp.float32)
    normed = (
        summit_wide
        * lax.rsqrt(jnp.mean(summit_wide * summit_wide, axis=1, keepdims=True) + 1e-05)
        * norm_gain
    ).astype(jnp.bfloat16)
    coarse_width = coarse_out.shape[0]
    head_count = coarse_width // HEAD_DIM
    projected = jnp.dot(
        normed,
        lax.all_gather(coarse_qkv, "sub", axis=1, tiled=True),
        preferred_element_type=jnp.float32,
    ).astype(jnp.bfloat16)
    head_queries = (
        projected[:, :coarse_width].reshape(top_count, head_count, HEAD_DIM).transpose(1, 0, 2)
    )
    query_top = device * top_count + jnp.arange(top_count, dtype=jnp.int32)
    key_rows = lax.all_gather(
        projected[:, coarse_width : 2 * coarse_width], ("ctx", "sub"), axis=0, tiled=True
    )
    value_rows = lax.all_gather(
        projected[:, 2 * coarse_width :], ("ctx", "sub"), axis=0, tiled=True
    )
    key_top = jnp.arange(key_rows.shape[0], dtype=jnp.int32)
    final_state = fold_block(
        empty_state(head_count, top_count),
        head_queries,
        key_rows,
        value_rows,
        key_top[None, :] <= query_top[:, None],
    )
    attended_top = finish_heads(final_state)
    lifted = jnp.dot(
        attended_top,
        lax.all_gather(coarse_out, "sub", axis=1, tiled=True),
        preferred_element_type=jnp.float32,
    ).astype(jnp.bfloat16)
    summit_sum = summit_rows.astype(jnp.float32) + lifted.astype(jnp.float32)
    middle_count = middle_rows.shape[0]
    widened = (
        middle_rows.astype(jnp.float32).reshape(top_count, SHORT, width)
        + up_coarse[None, :, :] * summit_sum[:, None, :]
    )
    widened = widened.reshape(middle_count, width)
    restored = (
        fine_stream.astype(jnp.float32).reshape(middle_count, SHORT, width)
        + up_fine[None, :, :] * widened[:, None, :]
    )
    return restored.reshape(local_rows, width).astype(jnp.bfloat16)


def solution(mesh):
    return jax.shard_map(
        shards,
        mesh=mesh,
        in_specs=(
            P(("ctx", "sub"), None),
            P(("ctx", "sub"), None),
            P(("ctx", "sub"), None),
            P(("ctx", "sub"), None),
            P(),
            P(),
            P(),
            P(),
            P(),
            P(None, "sub"),
            P(None, "sub"),
        ),
        out_specs=P(("ctx", "sub"), None),
        check_vma=False,
    )
```

profile of v0, /device:TPU:29, one launch (start us, length us, event | category | flops | bytes accessed | tf_op | source)
XLA Modules:
  0.0 800.8 jit_solution(8769069154204938152)
XLA Ops:
  6.5 1.5 copy.38
  9.6 6.2 collective-permute-start
  15.9 6.5 collective-permute-start.1
  22.4 1.9 collective-permute-start.2
  24.3 2.9 collective-permute-start.3
  27.2 2.1 collective-permute-start.4
  30.9 110.7 %collective-permute-done = bf16[2,256,1536]{1,2,0:T(8,128)(2,1)} collective-permute-done((bf16[2,256,1536]{1,2,0:T(8,128)(2,1)}, bf16[2,256,1536]{1,2,0:T(8,128)(2,1)}, u32[]{:S(2)}, u32[]{:S(2)}) %collective-permute-start) | collective-permute-done | bytes 1572896 | tf_op jit(solution)/shard_map/ppermute | solution.py:20
  141.6 8.7 %collective-permute-start.5 = (bf16[2,256,1536]{1,2,0:T(8,128)(2,1)}, bf16[2,256,1536]{1,2,0:T(8,128)(2,1)S(1)}, u32[]{:S(2)}, u32[]{:S(2)}) collective-permute-start(bf16[2,256,1536]{1,2,0:T(8,128)(2,1)} %pad_maximum_fusion), channel_id=1, source_target_pairs={{0,1},{1,2},{2,3},{3,4},{4,5},{5,6},{6,7},{7,8},{8,9},{9,10},{10,1... | collective-permute-start | bytes 4718600 | tf_op jit(solution)/shard_map/ppermute | solution.py:20
  150.3 2.7 constant_dynamic-update-slice_fusion.7
  153.0 85.5 %collective-permute-done.1 = bf16[2,256,1536]{1,2,0:T(8,128)(2,1)} collective-permute-done((bf16[2,256,1536]{1,2,0:T(8,128)(2,1)}, bf16[2,256,1536]{1,2,0:T(8,128)(2,1)}, u32[]{:S(2)}, u32[]{:S(2)}) %collective-permute-start.1) | collective-permute-done | bytes 1572896 | tf_op jit(solution)/shard_map/ppermute | solution.py:20
  238.5 2.7 constant_dynamic-update-slice_fusion.6
  241.3 40.9 %collective-permute-done.2 = bf16[2,256,1536]{1,2,0:T(8,128)(2,1)} collective-permute-done((bf16[2,256,1536]{1,2,0:T(8,128)(2,1)}, bf16[2,256,1536]{1,2,0:T(8,128)(2,1)}, u32[]{:S(2)}, u32[]{:S(2)}) %collective-permute-start.2) | collective-permute-done | bytes 1572896 | tf_op jit(solution)/shard_map/ppermute | solution.py:20
  282.2 2.7 constant_dynamic-update-slice_fusion.5
  284.9 70.5 %collective-permute-done.3 = bf16[2,256,1536]{1,2,0:T(8,128)(2,1)} collective-permute-done((bf16[2,256,1536]{1,2,0:T(8,128)(2,1)}, bf16[2,256,1536]{1,2,0:T(8,128)(2,1)}, u32[]{:S(2)}, u32[]{:S(2)}) %collective-permute-start.3) | collective-permute-done | bytes 1572896 | tf_op jit(solution)/shard_map/ppermute | solution.py:20
  355.4 2.7 constant_dynamic-update-slice_fusion.4
  358.2 31.1 %collective-permute-done.4 = bf16[2,256,1536]{1,2,0:T(8,128)(2,1)} collective-permute-done((bf16[2,256,1536]{1,2,0:T(8,128)(2,1)}, bf16[2,256,1536]{1,2,0:T(8,128)(2,1)}, u32[]{:S(2)}, u32[]{:S(2)}) %collective-permute-start.4) | collective-permute-done | bytes 1572896 | tf_op jit(solution)/shard_map/ppermute | solution.py:20
  389.2 2.8 constant_dynamic-update-slice_fusion.3
  392.0 11.8 %collective-permute-done.5 = bf16[2,256,1536]{1,2,0:T(8,128)(2,1)S(1)} collective-permute-done((bf16[2,256,1536]{1,2,0:T(8,128)(2,1)}, bf16[2,256,1536]{1,2,0:T(8,128)(2,1)S(1)}, u32[]{:S(2)}, u32[]{:S(2)}) %collective-permute-start.5) | collective-permute-done | bytes 1572896 | tf_op jit(solution)/shard_map/ppermute | solution.py:20
  406.4 9.0 %fusion.45 = (bf16[1,1792,1536]{1,2,0:T(8,128)(2,1)}, bf16[1,1792,1536]{1,2,0:T(8,128)(2,1)}) fusion(bf16[2,1792,1536]{1,2,0:T(8,128)(2,1)} %constant_dynamic-update-slice_fusion.1), kind=kLoop, calls=%fused_computation.80 | loop fusion | bytes 22020096 | tf_op jit(solution)/shard_map/slice | solution.py:118
  415.4 62.2 %while.11 = (s32[]{:T(128)}, f32[12,256,128]{1,2,0:T(8,128)}, bf16[12,256,128]{1,2,0:T(8,128)(2,1)}, bf16[12,1792,128]{1,2,0:T(8,128)(2,1)}, bf16[12,1792,128]{1...) while((s32[]{:T(128)}, f32[12,256,128]{1,2,0:T(8,128)}, ...), condition=%wide.region_3.4_spmd.clone, body=%wide.region_0.3_spmd.clone.sunk | while | flops 244547072 | bytes 7183717 | solution.py:119
  415.4 1.8 fusion.58
  418.1 1.8 fusion.60
  420.6 1.8 fusion.58
  423.3 1.8 fusion.60
  425.8 1.8 fusion.58
  428.4 1.8 fusion.60
  431.0 1.8 fusion.58
  433.6 1.8 fusion.60
  436.2 1.8 fusion.58
  438.8 1.8 fusion.60
  441.4 1.8 fusion.58
  444.0 1.8 fusion.60
  446.6 1.8 fusion.58
  449.2 1.8 fusion.60
  451.7 1.8 fusion.58
  454.4 1.8 fusion.60
  456.9 1.8 fusion.58
  459.6 1.8 fusion.60
  462.1 1.8 fusion.58
  464.8 1.8 fusion.60
  467.3 1.8 fusion.58
  470.0 1.8 fusion.60
  472.5 1.8 fusion.58
  475.1 1.8 fusion.60
  477.7 1.6 fusion.21
  479.4 4.3 collective-permute-start.6
  483.7 4.7 collective-permute-done.6
  488.4 1.5 fusion.28
  489.9 1.9 copy.44
  491.8 1.6 reshape.124
  493.5 2.5 multiply_reduce_fusion
  496.0 4.4 collective-permute-start.7
  500.4 3.1 collective-permute-done.7
  504.0 4.9 convolution_convert_fusion
  511.1 117.7 %all-gather.7.cloned.1.call-done = bf16[4096,768]{1,0:T(8,128)(2,1)} async-done(((bf16[16,768]{1,0:T(8,128)(2,1)}), bf16[4096,768]{1,0:T(8,128)(2,1)}) %all-gather.7.cloned.1.call-update) | async-done | bytes 6291472 | tf_op jit(solution)/shard_map/all_gather | solution.py:152
  628.8 8.7 %copy.46 = bf16[4096,768]{0,1:T(8,128)(2,1)} copy(bf16[4096,768]{1,0:T(8,128)(2,1)} %all-gather.7.cloned.1.call-done) | data formatting | bytes 12582912 | tf_op jit(solution)/shard_map/all_gather | solution.py:152
  637.5 108.6 %all-gather.9.cloned.1.call-done = bf16[4096,768]{1,0:T(8,128)(2,1)} async-done(((bf16[16,768]{1,0:T(8,128)(2,1)}), bf16[4096,768]{1,0:T(8,128)(2,1)}) %all-gather.9.cloned.1.call-update) | async-done | bytes 6291472 | tf_op jit(solution)/shard_map/all_gather | solution.py:155
  746.0 8.6 %copy.48 = bf16[4096,768]{0,1:T(8,128)(2,1)} copy(bf16[4096,768]{1,0:T(8,128)(2,1)} %all-gather.9.cloned.1.call-done) | data formatting | bytes 12582912 | tf_op jit(solution)/shard_map/all_gather | solution.py:155
  754.6 4.0 fusion.46
  759.4 1.8 fusion.26
  761.1 25.2 %all-gather.11.cloned.1.call-done = bf16[768,1536]{0,1:T(8,128)(2,1)} async-done(((bf16[768,96]{0,1:T(8,128)(2,1)}), bf16[768,1536]{0,1:T(8,128)(2,1)}) %all-gather.11.cloned.1.call-update) | async-done | bytes 2359312 | tf_op jit(solution)/shard_map/all_gather | solution.py:169
  786.4 2.4 fusion.20
  789.3 1.7 mul.115
  791.0 1.9 copy.51
  (94 shorter events, 30.0 us)
Async XLA Ops:
  6.5 1.5 copy-start
  6.5 497.5 %all-gather.5.cloned.1.call-start = ((), (), s32[]{:S(2)}) async-start(), calls=%async_computation | async-start | bytes 7520256 | tf_op jit(solution)/shard_map/all_gather | solution.py:145
  8.3 21.1 %copy-start.1 = (bf16[256,1536]{1,0:T(8,128)(2,1)S(1)}, bf16[256,1536]{1,0:T(8,128)(2,1)}, u32[]{:S(2)}) copy-start(bf16[256,1536]{1,0:T(8,128)(2,1)} %param.14) | copy-start | bytes 2359300
  8.3 22.3 %copy-start.2 = (bf16[256,1536]{1,0:T(8,128)(2,1)S(1)}, bf16[256,1536]{1,0:T(8,128)(2,1)}, u32[]{:S(2)}) copy-start(bf16[256,1536]{1,0:T(8,128)(2,1)} %param.13) | copy-start | bytes 2359300
  9.6 131.9 %collective-permute-start = (bf16[2,256,1536]{1,2,0:T(8,128)(2,1)}, bf16[2,256,1536]{1,2,0:T(8,128)(2,1)}, u32[]{:S(2)}, u32[]{:S(2)}) collective-permute-start(bf16[2,256,1536]{1,2,0:T(8,128)(2,1)} %pad_maximum_fusion), channel_id=1, source_target_pairs={{0,6},{1,7},{2,8},{3,9},{4,10},{5,11},{6,12},{7,13},{8,14},{9,15},... | collective-permute-start | bytes 4718600 | tf_op jit(solution)/shard_map/ppermute | solution.py:20
  15.9 222.6 %collective-permute-start.1 = (bf16[2,256,1536]{1,2,0:T(8,128)(2,1)}, bf16[2,256,1536]{1,2,0:T(8,128)(2,1)}, u32[]{:S(2)}, u32[]{:S(2)}) collective-permute-start(bf16[2,256,1536]{1,2,0:T(8,128)(2,1)} %pad_maximum_fusion), channel_id=1, source_target_pairs={{0,5},{1,6},{2,7},{3,8},{4,9},{5,10},{6,11},{7,12},{8,13},{9,14},{... | collective-permute-start | bytes 4718600 | tf_op jit(solution)/shard_map/ppermute | solution.py:20
  22.4 259.8 %collective-permute-start.2 = (bf16[2,256,1536]{1,2,0:T(8,128)(2,1)}, bf16[2,256,1536]{1,2,0:T(8,128)(2,1)}, u32[]{:S(2)}, u32[]{:S(2)}) collective-permute-start(bf16[2,256,1536]{1,2,0:T(8,128)(2,1)} %pad_maximum_fusion), channel_id=1, source_target_pairs={{0,4},{1,5},{2,6},{3,7},{4,8},{5,9},{6,10},{7,11},{8,12},{9,13},{1... | collective-permute-start | bytes 4718600 | tf_op jit(solution)/shard_map/ppermute | solution.py:20
  24.3 331.1 %collective-permute-start.3 = (bf16[2,256,1536]{1,2,0:T(8,128)(2,1)}, bf16[2,256,1536]{1,2,0:T(8,128)(2,1)}, u32[]{:S(2)}, u32[]{:S(2)}) collective-permute-start(bf16[2,256,1536]{1,2,0:T(8,128)(2,1)} %pad_maximum_fusion), channel_id=1, source_target_pairs={{0,3},{1,4},{2,5},{3,6},{4,7},{5,8},{6,9},{7,10},{8,11},{9,12},{10... | collective-permute-start | bytes 4718600 | tf_op jit(solution)/shard_map/ppermute | solution.py:20
  27.2 362.0 %collective-permute-start.4 = (bf16[2,256,1536]{1,2,0:T(8,128)(2,1)}, bf16[2,256,1536]{1,2,0:T(8,128)(2,1)}, u32[]{:S(2)}, u32[]{:S(2)}) collective-permute-start(bf16[2,256,1536]{1,2,0:T(8,128)(2,1)} %pad_maximum_fusion), channel_id=1, source_target_pairs={{0,2},{1,3},{2,4},{3,5},{4,6},{5,7},{6,8},{7,9},{8,10},{9,11},{10,... | collective-permute-start | bytes 4718600 | tf_op jit(solution)/shard_map/ppermute | solution.py:20
  29.3 599.4 %all-gather.7.cloned.1.call-start = ((), (), s32[]{:S(2)}) async-start(), calls=%async_computation.1 | async-start | bytes 6316032 | tf_op jit(solution)/shard_map/all_gather | solution.py:152
  141.6 262.2 %collective-permute-start.5 = (bf16[2,256,1536]{1,2,0:T(8,128)(2,1)}, bf16[2,256,1536]{1,2,0:T(8,128)(2,1)S(1)}, u32[]{:S(2)}, u32[]{:S(2)}) collective-permute-start(bf16[2,256,1536]{1,2,0:T(8,128)(2,1)} %pad_maximum_fusion), channel_id=1, source_target_pairs={{0,1},{1,2},{2,3},{3,4},{4,5},{5,6},{6,7},{7,8},{8,9},{9,10},{10,1... | collective-permute-start | bytes 4718600 | tf_op jit(solution)/shard_map/ppermute | solution.py:20
  479.4 9.0 %collective-permute-start.6 = (bf16[3,1536]{0,1:T(8,128)(2,1)S(1)}, bf16[3,1536]{0,1:T(8,128)(2,1)S(1)}, u32[]{:S(2)}, u32[]{:S(2)}) collective-permute-start(bf16[3,1536]{0,1:T(8,128)(2,1)S(1)} %slice.38), channel_id=1, source_target_pairs={{0,1},{1,2},{2,3},{3,4},{4,5},{5,6},{6,7},{7,8},{8,9},{9,10},{10,1... | collective-permute-start | bytes 27656 | tf_op jit(solution)/shard_map/ppermute | solution.py:20
  491.8 1.6 copy-start.3
  493.5 10.1 %copy-start.5 = (f32[4,1536]{1,0:T(4,128)S(1)}, f32[4,1536]{1,0:T(4,128)}, u32[]{:S(2)}) copy-start(f32[4,1536]{1,0:T(4,128)} %param.18) | copy-start | bytes 73732
  493.5 10.6 %copy-start.7 = (f32[1536]{0:T(1024)S(1)}, f32[1536]{0:T(1024)}, u32[]{:S(2)}) copy-start(f32[1536]{0:T(1024)} %param.21) | copy-start | bytes 18436
  496.0 7.5 collective-permute-start.7
  509.6 236.4 %all-gather.9.cloned.1.call-start = ((), (), s32[]{:S(2)}) async-start(), calls=%async_computation.2 | async-start | bytes 6316032 | tf_op jit(solution)/shard_map/all_gather | solution.py:155
  510.4 276.0 %all-gather.11.cloned.1.call-start = ((), (), s32[]{:S(2)}) async-start(), calls=%async_computation.3 | async-start | bytes 2506752 | tf_op jit(solution)/shard_map/all_gather | solution.py:169
  754.6 4.4 slice-start
  754.6 4.8 slice-start.1
  761.1 27.6 %copy-start.6 = (f32[4,1536]{1,0:T(4,128)S(1)}, f32[4,1536]{1,0:T(4,128)}, u32[]{:S(2)}) copy-start(f32[4,1536]{1,0:T(4,128)} %param.20) | copy-start | bytes 73732
  761.1 27.9 %copy-start.4 = (f32[4,1536]{1,0:T(4,128)S(1)}, f32[4,1536]{1,0:T(4,128)}, u32[]{:S(2)}) copy-start(f32[4,1536]{1,0:T(4,128)} %param.19) | copy-start | bytes 73732
Sparse Core Ops, SparseCore 0:
  29.5 148.0 all-gather.4
  509.8 118.9 all-gather.6
  632.6 113.3 all-gather.8
  747.7 38.5 all-gather.10
where the time goes:
time: 804 us; the launch traced here: 801 us
  waiting for transfers between devices  611 us (76%)
  local copies, waits for them, and re-layouts  63.2 us (8%)
  matrix products  56.3 us (7%)
  starting transfers between devices  37.3 us (5%)
  other arithmetic  19.4 us (2%)
  between operations  13.4 us (2%)
    ppermute x8, waiting for transfers between devices, shifted(): return lax.ppermute(value, axis, pairs)  358 us
    all_gather x1, waiting for transfers between devices, shards(): lax.all_gather(projected[:, coarse_width:2 * coarse_width], ('ctx', 'sub'...  118 us
    all_gather x1, waiting for transfers between devices, shards(): lax.all_gather(projected[:, 2 * coarse_width:], ('ctx', 'sub'), axis=0, t...  109 us
    ppermute x8, starting transfers between devices, shifted(): return lax.ppermute(value, axis, pairs)  37 us
    all_gather x1, waiting for transfers between devices, shards(): lax.all_gather(coarse_out, 'sub', axis=1, tiled=True)  25.2 us
    dot_general x12, matrix products, head_output(): jnp.dot(query_one, key_one.T, preferred_element_type=jnp.float32)  22 us
    dot_general x12, matrix products, head_output(): jnp.dot(weights.astype(jnp.bfloat16), value_one, preferred_element_type=j...  21.3 us
    unnamed x31, local copies, waits for them, and re-layouts  19.2 us
  transfers between devices with their start and end apart: 12, of which 11 were waited for; matrix products, arithmetic and copies ran while one was open for 15% of the time, Pallas kernels for 0%

commit v1 on v0

v1 whole, which is shorter than its diff:
```python
import functools
import math

import jax
import jax.numpy as jnp
from jax import lax
from jax.experimental import pallas as pl
from jax.experimental.pallas import tpu as pltpu
from jax.sharding import PartitionSpec as P

MESH = pl.DeviceIdType.MESH
F32 = jnp.float32
BF16 = jnp.bfloat16

HEADS = 12
CHEADS = 6
HD = 128
SHORT = 4
ROWS = 256
HALF = 128
REACH = 6
CHUNKS = 2 * HEADS
SPAN = 2 * REACH
WIDTH = HEADS * HD
OROWS = HD + 16
LEAD = 24
MROWS = 72
QKV_COLS = 144
OUT_COLS = 96
UNIT = 16
SCALE = math.log2(math.e) / math.sqrt(HD)
NEG = -float(2**100)


def nt(a, b):
    return lax.dot_general(a, b, (((1,), (1,)), ((), ())), preferred_element_type=F32)


def dot(a, b):
    return jnp.dot(a, b, preferred_element_type=F32)


def rounded(x):
    return x.astype(BF16).astype(F32)


def kernel(
    n_ctx, n_sub,
    q_ref, k_ref, v_ref, x_ref, pf_ref, pc_ref, uf_ref, uc_ref, ng_ref, wq_ref, wo_ref,
    out_ref,
    qbuf, oin, oout, vt, fine, ebuf, edge, mid, summit, normed, na, wqs, wos, pt, hb,
    kb, vb, osc, ah, ls, lb,
    q_send, q_recv, o_send, o_recv, e_send, e_recv, w_send, w_recv,
    n_send, n_recv, u_send, u_recv, k_send, k_recv, v_send, v_recv, a_send, a_recv, l_send, l_recv,
):
    ctx = lax.axis_index("ctx")
    sub = lax.axis_index("sub")
    n_all = n_ctx * n_sub
    n_chip = n_sub // 2
    me = ctx * n_sub + sub
    zc = sub // 2
    core = sub % 2
    left = (me + n_all - 1) % n_all
    right = (me + 1) % n_all
    left_id = (left // n_sub, left % n_sub)
    right_id = (right // n_sub, right % n_sub)

    barrier = pltpu.get_barrier_semaphore()

    def greet(device):
        pl.semaphore_signal(barrier, inc=1, device_id=device, device_id_type=MESH)

    greet(left_id)
    greet(right_id)
    for step in range(1, n_sub):
        greet((ctx, (sub + step) % n_sub))
    for step in range(1, n_ctx):
        greet(((ctx + step) % n_ctx, sub))

    for h in range(HEADS):
        vt[h] = v_ref[:, h * HD : (h + 1) * HD].astype(F32).T.astype(BF16)

    pl.semaphore_wait(barrier, 2 + (n_sub - 1) + (n_ctx - 1))

    def remote(src, dst, send, recv, device):
        return pltpu.make_async_remote_copy(
            src_ref=src, dst_ref=dst, send_sem=send, recv_sem=recv,
            device_id=device, device_id_type=MESH,
        )

    sibling = (ctx, 2 * zc)

    def weight_copies():
        return (
            remote(wq_ref, wqs, w_send.at[0], w_recv.at[0], sibling),
            remote(wo_ref, wos, w_send.at[1], w_recv.at[1], sibling),
        )

    @pl.when(core == 1)
    def _():
        for copy in weight_copies():
            copy.start()

    def lanes(h):
        return pl.ds(pl.multiple_of(h * HD, HD), HD)

    def own_rows(half):
        return pl.ds(pl.multiple_of(half * HALF, HALF), HALF)

    def q_copy(s, g):
        if s == 0:
            src = q_ref.at[own_rows(g % 2), lanes(g // 2)]
        else:
            src = qbuf.at[s - 1, g]
        return remote(src, qbuf.at[s, g], q_send.at[s, g % 2], q_recv.at[s, g], left_id)

    def o_copy(s, g):
        return remote(
            oout.at[s - 1, g % 2], oin.at[s - 1, g], o_send.at[s - 1, g % 2], o_recv.at[s - 1, g], right_id
        )

    def edge_copy(h):
        return remote(ebuf.at[:, lanes(h)], edge.at[:, lanes(h)], e_send.at[0], e_recv.at[0], right_id)

    def forward(i, s, g):
        if s > 0:
            q_copy(s - 1, g).wait_recv()

        @pl.when(g >= 2)
        def _():
            q_copy(s, g - 2).wait_send()

        q_copy(s, g).start()

    def partial(s, g):
        h, half = g // 2, g % 2
        keys = k_ref[:, lanes(h)]
        queries = q_ref[own_rows(half), lanes(h)] if s == 0 else qbuf[s - 1, g]
        t = nt(keys, queries) * SCALE
        if s == 0 or s == REACH:
            key_row = lax.broadcasted_iota(jnp.int32, t.shape, 0)
            query_row = lax.broadcasted_iota(jnp.int32, t.shape, 1) + half * HALF
            t = jnp.where(key_row <= query_row if s == 0 else key_row > query_row, t, NEG)
        peak = rounded(jnp.max(t, axis=0, keepdims=True))
        p = jnp.exp2(t - peak)
        total = jnp.sum(p, axis=0, keepdims=True)
        summed = dot(vt[h], p.astype(BF16))
        if s > 0:
            peak = jnp.where(me + s < n_all, peak, NEG)
        return peak, total, summed

    def settle(s, g, state):
        h, half = g // 2, g % 2
        peak, total, summed = state
        if s < REACH:
            o_copy(s + 1, g).wait_recv()
            stats = oin[s, g, HD:OROWS, :].astype(F32)
            before = stats[0:1]
            top = jnp.maximum(before, peak)
            a = jnp.exp2(before - top)
            b = jnp.exp2(peak - top)
            summed = oin[s, g, 0:HD, :].astype(F32) * a + summed * b
            total = (stats[1:2] + stats[2:3]) * a + total * b
            peak = top
        if s > 0:
            slot = g % 2

            @pl.when(g >= 2)
            def _():
                o_copy(s, g - 2).wait_send()

            oout[s - 1, slot, 0:HD, :] = summed.astype(BF16)
            high = rounded(total)
            row = lax.broadcasted_iota(jnp.int32, (16, HALF), 0)
            stats = jnp.where(row == 0, peak, jnp.where(row == 1, high, total - high))
            oout[s - 1, slot, HD:OROWS, :] = stats.astype(BF16)
            o_copy(s, g).start()
        else:
            attended = (summed / total).T
            base = x_ref[own_rows(half), lanes(h)].astype(F32)
            rows16 = (base + attended).astype(BF16)
            fine[h, pl.ds(pl.multiple_of(LEAD + half * HALF, 8), HALF), :] = rows16.astype(F32)

            @pl.when(half == 1)
            def _():
                ebuf[:, lanes(h)] = rows16[HALF - 16 :, :]
                edge_copy(h).start()

    def guarded(i, steps_q, steps_o):
        for s in steps_q:
            g = i - s

            @pl.when((g >= 0) & (g < CHUNKS))
            def _(s=s, g=g):
                forward(i, s, g)

        for s in steps_o:
            g = i - SPAN + s

            @pl.when((g >= 0) & (g < CHUNKS))
            def _(s=s, g=g):
                if s == REACH:
                    q_copy(s - 1, g).wait_recv()
                settle(s, g, partial(s, g))

    def ramp_up(i, carry):
        guarded(i, range(REACH), range(REACH, -1, -1))
        return carry

    def steady(i, carry):
        for s in range(REACH):
            g = i - s

            @pl.when(g < CHUNKS)
            def _(s=s, g=g):
                forward(i, s, g)

        q_copy(REACH - 1, i - REACH).wait_recv()
        states = {s: partial(s, i - SPAN + s) for s in range(REACH, -1, -1)}
        for s in range(REACH, -1, -1):
            settle(s, i - SPAN + s, states[s])
        return carry

    def ramp_down(i, carry):
        guarded(i, (), range(REACH - 1, -1, -1))
        return carry

    lax.fori_loop(0, SPAN, ramp_up, 0)
    lax.fori_loop(SPAN, CHUNKS + REACH, steady, 0)
    lax.fori_loop(CHUNKS + REACH, CHUNKS + SPAN, ramp_down, 0)

    for s in range(REACH):
        for slot in range(2):
            q_copy(s, CHUNKS - 2 + slot).wait_send()
            o_copy(s + 1, CHUNKS - 2 + slot).wait_send()

    whole_edge = remote(ebuf, edge, e_send.at[0], e_recv.at[0], right_id)
    whole_edge.wait_recv()
    square = jnp.zeros((16, 1), F32)
    for h in range(HEADS):
        at = slice(h * HD, (h + 1) * HD)
        fine[h, 0:8, :] = jnp.zeros((8, HD), F32)
        fine[h, 8:LEAD, :] = jnp.where(me > 0, edge[:, at].astype(F32), 0.0)
        row = jnp.zeros((68, HD), F32)
        for k in range(SHORT):
            row = row + fine[h, pl.ds(LEAD - 19 + k, 68, stride=SHORT), :] * pf_ref[k : k + 1, at]
        mid[h, 0:68, :] = rounded(row)
        row = jnp.zeros((16, HD), F32)
        for k in range(SHORT):
            row = row + mid[h, pl.ds(1 + k, 16, stride=SHORT), :] * pc_ref[k : k + 1, at]
        row = rounded(row)
        summit[:, at] = row
        square = square + jnp.sum(row * row, axis=1, keepdims=True)
    whole_edge.wait_send()
    normed[...] = (summit[...] * lax.rsqrt(square / WIDTH + 1e-05) * ng_ref[...]).astype(BF16)

    def n_copy(step):
        target = (zc + step) % n_chip
        return remote(normed, na.at[sub], n_send.at[step], n_recv.at[sub], (ctx, 2 * target))

    def n_arrival(source):
        return remote(normed, na.at[source], n_send.at[0], n_recv.at[source], sibling)

    for step in range(1, n_chip):
        n_copy(step).start()

    @pl.when(core == 1)
    def _():
        n_copy(0).start()

    def u_copy(i, head, dest):
        unit = 18 * zc + i
        piece = unit // 8
        at = pl.multiple_of((piece // CHEADS) * HD + (unit % 8) * UNIT, UNIT)
        return pt.at[pl.ds(i * UNIT, UNIT)], hb.at[pl.ds(at, UNIT)]

    def spread(i):
        unit = 18 * zc + i
        piece = unit // 8
        head = piece % CHEADS
        src, dst = u_copy(i, head, None)
        return head, remote(src, dst, u_send.at[i], u_recv.at[0], (ctx, 2 * head)), pltpu.make_async_copy(src, dst, u_recv.at[0])

    def k_copy(source, step):
        return remote(kb.at[source], kb.at[source], k_send.at[step], k_recv.at[source], (source + step, sub))

    def v_copy(source, step):
        return remote(vb.at[source], vb.at[source], v_send.at[step], v_recv.at[source], (source + step, sub))

    def a_copy(step):
        return remote(ah.at[zc], ah.at[zc], a_send.at[step], a_recv.at[zc], (ctx, 2 * ((zc + step) % n_chip)))

    def l_copy(step):
        target = (sub + step) % n_sub
        rows = pl.ds(pl.multiple_of(target * UNIT, UNIT), UNIT)
        return remote(ls.at[:, rows, :], lb.at[zc], l_send.at[step], l_recv.at[zc], (ctx, target))

    @pl.when(core == 0)
    def _():
        na[sub] = normed[...]
        for copy in weight_copies():
            copy.wait_recv()
        for source in range(n_sub):
            @pl.when(source != sub)
            def _(source=source):
                n_arrival(source).wait_recv()
        rows = na[...].reshape(ROWS, WIDTH)
        pad = jnp.zeros((ROWS, ROWS - QKV_COLS), F32)
        for place, w in enumerate((wq_ref, wqs)):
            wide = jnp.concatenate([dot(rows, w[...]), pad], axis=1).T
            pt[place * QKV_COLS : (place + 1) * QKV_COLS, :] = wide[:QKV_COLS].astype(BF16)
        for i in range(18):
            head, away, here = spread(i)

            @pl.when(head == zc)
            def _(here=here):
                here.start()

            @pl.when(head != zc)
            def _(away=away):
                away.start()

    @pl.when((core == 0) & (zc < CHEADS))
    def _():
        pltpu.make_async_copy(hb, hb, u_recv.at[0]).wait()
        queries = hb[0:HD].astype(F32).T.astype(BF16)
        kb[ctx] = hb[HD : 2 * HD].astype(F32).T.astype(BF16)
        vb[ctx] = hb[2 * HD : 3 * HD]
        for step in range(1, n_ctx):
            @pl.when(ctx + step < n_ctx)
            def _(step=step):
                k_copy(ctx, step).start()
                v_copy(ctx, step).start()

        t = nt(kb[ctx], queries) * SCALE
        key_row = lax.broadcasted_iota(jnp.int32, t.shape, 0)
        query_row = lax.broadcasted_iota(jnp.int32, t.shape, 1)
        t = jnp.where(key_row <= query_row, t, NEG)
        peak = jnp.max(t, axis=0, keepdims=True)
        p = jnp.exp2(t - peak)
        total = jnp.sum(p, axis=0, keepdims=True)
        osc[...] = dot(vb[ctx], p.astype(BF16))

        def fold(i, carry):
            before, total = carry
            source = ctx - 1 - i
            k_copy(source, 1).wait_recv()
            v_copy(source, 1).wait_recv()
            t = nt(kb[source], queries) * SCALE
            peak = jnp.maximum(before, jnp.max(t, axis=0, keepdims=True))
            p = jnp.exp2(t - peak)
            a = jnp.exp2(before - peak)
            osc[...] = osc[...] * a + dot(vb[source], p.astype(BF16))
            return peak, total * a + jnp.sum(p, axis=0, keepdims=True)

        peak, total = lax.fori_loop(0, ctx, fold, (peak, total))
        ah[zc] = (osc[...] / total).T.astype(BF16)
        for step in range(1, n_chip):
            a_copy(step).start()

    @pl.when(core == 0)
    def _():
        for head in range(CHEADS):
            @pl.when(head != zc)
            def _(head=head):
                remote(ah.at[head], ah.at[head], a_send.at[0], a_recv.at[head], sibling).wait_recv()
        pad = jnp.zeros((ROWS, HD - OUT_COLS), F32)
        for place, w in enumerate((wo_ref, wos)):
            lifted = dot(ah[0], w[0:HD, :])
            for head in range(1, CHEADS):
                lifted = lifted + dot(ah[head], w[head * HD : (head + 1) * HD, :])
            ls[place] = jnp.concatenate([lifted, pad], axis=1).astype(BF16)
        for step in range(1, n_sub):
            l_copy(step).start()
        lb[zc] = ls[:, pl.ds(pl.multiple_of(sub * UNIT, UNIT), UNIT), :]

    for chip in range(n_chip):
        @pl.when((core == 1) | (chip != zc))
        def _(chip=chip):
            remote(ls.at[:, 0:UNIT, :], lb.at[chip], l_send.at[0], l_recv.at[chip], sibling).wait_recv()

    pieces = []
    for chip in range(n_chip):
        for place in range(2):
            pieces.append(lb[chip, place].astype(F32)[:, :OUT_COLS])
    summit[...] = summit[...] + jnp.concatenate(pieces, axis=1)

    for h in range(HEADS):
        at = slice(h * HD, (h + 1) * HD)
        lift = summit[:, at]
        for k in range(SHORT):
            place = pl.ds(4 + k, 16, stride=SHORT)
            mid[h, place, :] = mid[h, place, :] + uc_ref[k : k + 1, at] * lift
        lift = mid[h, 4:68, :]
        for k in range(SHORT):
            place = pl.ds(LEAD + k, 64, stride=SHORT)
            fine[h, place, :] = fine[h, place, :] + uf_ref[k : k + 1, at] * lift
        out_ref[:, at] = fine[h, LEAD : LEAD + ROWS, :].astype(BF16)

    whole_edge_done = None
    @pl.when(core == 1)
    def _():
        for copy in weight_copies():
            copy.wait_send()
        n_copy(0).wait_send()

    for step in range(1, n_chip):
        n_copy(step).wait_send()

    @pl.when(core == 0)
    def _():
        for i in range(18):
            head, away, here = spread(i)

            @pl.when(head != zc)
            def _(away=away):
                away.wait_send()
        for step in range(1, n_sub):
            l_copy(step).wait_send()

    @pl.when((core == 0) & (zc < CHEADS))
    def _():
        for step in range(1, n_ctx):
            @pl.when(ctx + step < n_ctx)
            def _(step=step):
                k_copy(ctx, step).wait_send()
                v_copy(ctx, step).wait_send()
        for step in range(1, n_chip):
            a_copy(step).wait_send()


def solution(mesh):
    n_ctx, n_sub = mesh.shape["ctx"], mesh.shape["sub"]
    n_chip = n_sub // 2
    dma = pltpu.SemaphoreType.DMA

    def shards(stream, q, k, v, pf, pc, uf, uc, ng, wq, wo):
        vmem = pl.BlockSpec(memory_space=pltpu.VMEM)
        return pl.pallas_call(
            functools.partial(kernel, n_ctx, n_sub),
            out_shape=jax.ShapeDtypeStruct((ROWS, WIDTH), BF16),
            in_specs=[vmem] * 11,
            out_specs=vmem,
            scratch_shapes=[
                pltpu.VMEM((REACH, CHUNKS, HALF, HD), BF16),
                pltpu.VMEM((REACH, CHUNKS, OROWS, HALF), BF16),
                pltpu.VMEM((REACH, 2, OROWS, HALF), BF16),
                pltpu.VMEM((HEADS, HD, ROWS), BF16),
                pltpu.VMEM((HEADS, LEAD + ROWS, HD), F32),
                pltpu.VMEM((16, WIDTH), BF16),
                pltpu.VMEM((16, WIDTH), BF16),
                pltpu.VMEM((HEADS, MROWS, HD), F32),
                pltpu.VMEM((16, WIDTH), F32),
                pltpu.VMEM((16, WIDTH), BF16),
                pltpu.VMEM((n_sub, 16, WIDTH), BF16),
                pltpu.VMEM(wq.shape, BF16),
                pltpu.VMEM(wo.shape, BF16),
                pltpu.VMEM((2 * QKV_COLS, ROWS), BF16),
                pltpu.VMEM((3 * HD, ROWS), BF16),
                pltpu.VMEM((n_ctx, ROWS, HD), BF16),
                pltpu.VMEM((n_ctx, HD, ROWS), BF16),
                pltpu.VMEM((HD, ROWS), F32),
                pltpu.VMEM((CHEADS, ROWS, HD), BF16),
                pltpu.VMEM((2, ROWS, HD), BF16),
                pltpu.VMEM((n_chip, 2, UNIT, HD), BF16),
                dma((REACH, 2)), dma((REACH, CHUNKS)),
                dma((REACH, 2)), dma((REACH, CHUNKS)),
                dma((1,)), dma((1,)),
                dma((2,)), dma((2,)),
                dma((n_chip,)), dma((n_sub,)),
                dma((18,)), dma((1,)),
                dma((n_ctx,)), dma((n_ctx,)),
                dma((n_ctx,)), dma((n_ctx,)),
                dma((n_chip,)), dma((CHEADS,)),
                dma((n_sub,)), dma((n_chip,)),
            ],
            compiler_params=pltpu.CompilerParams(
                collective_id=0, has_side_effects=True, vmem_limit_bytes=60 * 2**20
            ),
        )(q, k, v, stream, pf, pc, uf, uc, ng.reshape(1, WIDTH), wq, wo)

    rows = P(("ctx", "sub"), None)
    return jax.shard_map(
        shards,
        mesh=mesh,
        in_specs=(rows, rows, rows, rows, P(), P(), P(), P(), P(), P(None, "sub"), P(None, "sub")),
        out_specs=rows,
        check_vma=False,
    )
```

time: 804 us -> 209 us (0.26)
  waiting for transfers between devices: 611 us -> 0 us
  Pallas kernels: 0 us -> 201 us
  matrix products: 56.3 us -> 0 us
  local copies, waits for them, and re-layouts: 63.2 us -> 7.24 us
  starting transfers between devices: 37.3 us -> 0 us
  other arithmetic: 19.4 us -> 0 us
  between operations: 13.4 us -> 0.01 us
    ppermute x8 -> x0, waiting for transfers between devices: 358 us -> none  [shifted(): return lax.ppermute(value, axis, pairs)]
    all_gather x4 -> x0, waiting for transfers between devices: 251 us -> none  [the longest x1 118 us: shards(): lax.all_gather(projected[:, coarse_width:2 * coarse_width], ('ctx', 'sub'...]
    pallas_call x0 -> x1, Pallas kernels: none -> 201 us  [shards(): pl.pallas_call(functools.partial(kernel, n_ctx, n_sub), out_shape=jax.Sha...]
    dot_general x28 -> x0, matrix products: 56.3 us -> none  [the longest x12 22 us: head_output(): jnp.dot(query_one, key_one.T, preferred_element_type=jnp.float32)]
    ppermute x8 -> x0, starting transfers between devices: 37 us -> none  [shifted(): return lax.ppermute(value, axis, pairs)]
    all_gather x2 -> x0, local copies, waits for them, and re-layouts: 17.2 us -> none  [the longest x1 8.69 us: shards(): lax.all_gather(projected[:, coarse_width:2 * coarse_width], ('ctx', 'sub'...]
    unnamed x31 -> x3, local copies, waits for them, and re-layouts: 19.2 us -> 5.95 us
    reduce_sum x16 -> x0, other arithmetic: 13 us -> none  [the longest x12 9.67 us: head_output(): total_sum = jnp.sum(weights, axis=1, keepdims=True)]
  transfers between devices with their start and end apart: 12 -> 0, of which waited for: 11 -> 0; matrix products, arithmetic and copies ran while one was open for 15% -> 0% of each run, Pallas kernels for 0% -> 0%
where the time goes in v1:
time: 209 us
  Pallas kernels  201 us (96%)
  local copies, waits for them, and re-layouts  7.24 us (3%)
    pallas_call x1, Pallas kernels, shards(): pl.pallas_call(functools.partial(kernel, n_ctx, n_sub), out_shape=jax.Sha...  201 us
    unnamed x3, local copies, waits for them, and re-layouts  5.95 us

profile of v1, /device:TPU:29, one launch (start us, length us, event | category | flops | bytes accessed | tf_op | source)
XLA Modules:
  0.0 208.7 jit_solution(1463174698420785532)
XLA Ops:
  0.0 1.3 reshape.3.ng_ref
  1.3 1.7 copy.13.wo_ref
  3.0 2.2 %copy.12.wq_ref = bf16[1536,144]{1,0:T(8,128)(2,1)} copy(bf16[1536,144]{0,1:T(8,128)(2,1)} %param.20) | data formatting | bytes 884736 | tf_op args[9]
  5.2 201.4 %shard_map.109 = bf16[256,1536]{1,0:T(8,128)(2,1)} custom-call(bf16[256,1536]{1,0:T(8,128)(2,1)} %q_ref.1, bf16[256,1536]{1,0:T(8,128)(2,1)} %k_ref.1, bf16[256,1536]{1,0:T(8,128)(2,1)} %v_ref.1, bf16[256,1536]{1,0:T(8,128)(2,1)} %x_ref.1, f32[4,1536]{1,0:T(4,128)} %pf_ref.1, f32[4,1536]{1,0:T(4,128)} %pc_ref.1, f32[4,1536]{1,0:T(4,128)} %uf_ref.1, ...), custom_call_target="tpu_custom_call" | custom-call | tf_op jit(solution)/shard_map/pallas_call | solution.py:439
  206.6 2.1 copy.15

commit v2 on v1

v2 whole, which is shorter than its diff:
```python
import functools
import math

import jax
import jax.numpy as jnp
from jax import lax
from jax.experimental import pallas as pl
from jax.experimental.pallas import tpu as pltpu
from jax.sharding import PartitionSpec as P

MESH = pl.DeviceIdType.MESH
F32 = jnp.float32
BF16 = jnp.bfloat16

HEADS = 12
CHEADS = 6
HD = 128
SHORT = 4
ROWS = 256
CHIP_ROWS = 2 * ROWS
OWN = HEADS // 2
HALF = 128
BLOCKS = CHIP_ROWS // HALF
REACH = 3
CHUNKS = OWN * BLOCKS
LAG = 2
SLOTS = 4
SPAN = 2 * REACH * LAG
WIDTH = HEADS * HD
OROWS = HD + 16
LEAD = 24
MROWS = 72
QKV_COLS = 144
OUT_COLS = 96
UNIT = 16
SCALE = math.log2(math.e) / math.sqrt(HD)
NEG = -float(2**100)


def nt(a, b):
    return lax.dot_general(a, b, (((1,), (1,)), ((), ())), preferred_element_type=F32)


def dot(a, b):
    return jnp.dot(a, b, preferred_element_type=F32)


def rounded(x):
    return x.astype(BF16).astype(F32)


def kernel(
    n_ctx, n_sub,
    q_ref, k_ref, v_ref, x_ref, pf_ref, pc_ref, uf_ref, uc_ref, ng_ref, wq_ref, wo_ref,
    out_ref,
    qx, kx, vx, xx, qbuf, oin, oout, vt, fout, fine, mid, summit, normed, na, wqs, wos, pt, hb,
    kb, vb, osc, ah, ls, lb,
    x_send, x_recv, q_send, q_recv, o_send, o_recv, f_send, f_recv, e_send, e_recv, w_send, w_recv,
    n_send, n_recv, u_send, u_recv, k_send, k_recv, v_send, v_recv, a_send, a_recv, l_send, l_recv,
):
    ctx = lax.axis_index("ctx")
    sub = lax.axis_index("sub")
    n_chip = n_sub // 2
    n_chips = n_ctx * n_chip
    me = ctx * n_sub + sub
    zc = sub // 2
    core = sub % 2
    other = 1 - core
    chip = ctx * n_chip + zc
    left = (chip + n_chips - 1) % n_chips
    right = (chip + 1) % n_chips
    left_id = (left // n_chip, 2 * (left % n_chip) + core)
    right_id = (right // n_chip, 2 * (right % n_chip) + core)
    right_first = (right // n_chip, 2 * (right % n_chip))
    twin = (ctx, 2 * zc + other)

    barrier = pltpu.get_barrier_semaphore()

    def greet(device):
        pl.semaphore_signal(barrier, inc=1, device_id=device, device_id_type=MESH)

    for near in (left, right):
        for side in range(2):
            greet((near // n_chip, 2 * (near % n_chip) + side))
    for step in range(1, n_sub):
        greet((ctx, (sub + step) % n_sub))
    for step in range(1, n_ctx):
        greet(((ctx + step) % n_ctx, sub))

    def remote(src, dst, send, recv, device):
        return pltpu.make_async_remote_copy(
            src_ref=src, dst_ref=dst, send_sem=send, recv_sem=recv,
            device_id=device, device_id_type=MESH,
        )

    own_rows = pl.ds(pl.multiple_of(core * ROWS, ROWS), ROWS)
    own_lanes = pl.ds(pl.multiple_of(core * OWN * HD, HD), OWN * HD)
    twin_lanes = pl.ds(pl.multiple_of(other * OWN * HD, HD), OWN * HD)
    parts = ((q_ref, qx), (k_ref, kx), (v_ref, vx), (x_ref, xx))
    for src, dst in parts:
        dst[own_rows, :] = src[:, own_lanes]

    def halves(n):
        src, dst = parts[n]
        return remote(src.at[:, twin_lanes], dst.at[own_rows], x_send.at[n], x_recv.at[n], twin)

    pl.semaphore_wait(barrier, 4 + (n_sub - 1) + (n_ctx - 1))
    for n in range(4):
        halves(n).start()

    sibling = (ctx, 2 * zc)

    def weight_copies():
        return (
            remote(wq_ref, wqs, w_send.at[0], w_recv.at[0], sibling),
            remote(wo_ref, wos, w_send.at[1], w_recv.at[1], sibling),
        )

    @pl.when(core == 1)
    def _():
        for copy in weight_copies():
            copy.start()

    def lanes(h):
        return pl.ds(pl.multiple_of(h * HD, HD), HD)

    def place(g):
        return g // BLOCKS, (g + 2 * core) % BLOCKS

    def block_rows(block):
        return pl.ds(pl.multiple_of(block * HALF, HALF), HALF)

    def q_copy(s, g):
        if s == 0:
            h, block = place(g)
            src = qx.at[block_rows(block), lanes(h)]
        else:
            src = qbuf.at[s - 1, g]
        return remote(src, qbuf.at[s, g], q_send.at[s, g % SLOTS], q_recv.at[s, g], left_id)

    def o_copy(s, g):
        return remote(
            oout.at[s - 1, g % SLOTS], oin.at[s - 1, g], o_send.at[s - 1, g % SLOTS],
            o_recv.at[s - 1, g], right_id,
        )

    def f_copy(h, half):
        head = core * OWN + h
        rows = pl.ds(pl.multiple_of(LEAD + half * HALF, 8), HALF)
        return remote(fout.at[h, half], fine.at[head, rows, :], f_send.at[h, half], f_recv.at[0], twin)

    def edge_of(h, device, slot):
        head = core * OWN + h
        return remote(
            fout.at[h, 2 + slot, pl.ds(HALF - 16, 16), :], fine.at[head, pl.ds(8, 16), :],
            e_send.at[h, slot], e_recv.at[0], device,
        )

    def forward(s, g):
        if s > 0:
            q_copy(s - 1, g).wait_recv()

        @pl.when(g >= SLOTS)
        def _():
            q_copy(s, g - SLOTS).wait_send()

        q_copy(s, g).start()

    def partial(s, g):
        h, block = place(g)
        keys = kx[:, lanes(h)]
        queries = qx[block_rows(block), lanes(h)] if s == 0 else qbuf[s - 1, g]
        t = nt(keys, queries) * SCALE
        if s == 0 or s == REACH:
            key_row = lax.broadcasted_iota(jnp.int32, t.shape, 0)
            query_row = lax.broadcasted_iota(jnp.int32, t.shape, 1) + block * HALF
            t = jnp.where(key_row <= query_row if s == 0 else key_row > query_row, t, NEG)
        peak = rounded(jnp.max(t, axis=0, keepdims=True))
        p = jnp.exp2(t - peak)
        total = jnp.sum(p, axis=0, keepdims=True)
        summed = dot(vt[h], p.astype(BF16))
        if s > 0:
            peak = jnp.where(chip + s < n_chips, peak, NEG)
        return peak, total, summed

    def settle(s, g, state):
        h, block = place(g)
        peak, total, summed = state
        if s < REACH:
            o_copy(s + 1, g).wait_recv()
            stats = oin[s, g, HD:OROWS, :].astype(F32)
            before = stats[0:1]
            top = jnp.maximum(before, peak)
            a = jnp.exp2(before - top)
            b = jnp.exp2(peak - top)
            summed = oin[s, g, 0:HD, :].astype(F32) * a + summed * b
            total = (stats[1:2] + stats[2:3]) * a + total * b
            peak = top
        if s > 0:
            slot = g % SLOTS

            @pl.when(g >= SLOTS)
            def _():
                o_copy(s, g - SLOTS).wait_send()

            oout[s - 1, slot, 0:HD, :] = summed.astype(BF16)
            high = rounded(total)
            row = lax.broadcasted_iota(jnp.int32, (16, HALF), 0)
            stats = jnp.where(row == 0, peak, jnp.where(row == 1, high, total - high))
            oout[s - 1, slot, HD:OROWS, :] = stats.astype(BF16)
            o_copy(s, g).start()
        else:
            attended = (summed / total).T
            base = xx[block_rows(block), lanes(h)].astype(F32)
            rows = rounded(base + attended)
            head = core * OWN + h
            half = block % 2

            @pl.when(block // 2 == core)
            def _():
                fine[head, pl.ds(pl.multiple_of(LEAD + half * HALF, 8), HALF), :] = rows

            @pl.when(block // 2 != core)
            def _():
                fout[h, half] = rows
                f_copy(h, half).start()

            @pl.when((block == 1) & (core == 1))
            def _():
                fine[head, 8:LEAD, :] = rows[HALF - 16 :, :]

            @pl.when((block == 1) & (core == 0))
            def _():
                fout[h, 2] = rows
                edge_of(h, twin, 0).start()

            @pl.when(block == 3)
            def _():
                fout[h, 3] = rows
                edge_of(h, right_first, 1).start()

    def guarded(i, steps_q, steps_o):
        for s in steps_q:
            g = i - s * LAG

            @pl.when((g >= 0) & (g < CHUNKS))
            def _(s=s, g=g):
                forward(s, g)

        for s in steps_o:
            g = i - (2 * REACH - s) * LAG

            @pl.when((g >= 0) & (g < CHUNKS))
            def _(s=s, g=g):
                if s == REACH:
                    q_copy(s - 1, g).wait_recv()
                settle(s, g, partial(s, g))

    def first(i, carry):
        guarded(i, range(REACH), ())
        return carry

    def ramp_up(i, carry):
        guarded(i, range(REACH), range(REACH, -1, -1))
        return carry

    def steady(i, carry):
        for s in range(REACH):
            g = i - s * LAG

            @pl.when(g < CHUNKS)
            def _(s=s, g=g):
                forward(s, g)

        at = {s: i - (2 * REACH - s) * LAG for s in range(REACH + 1)}
        q_copy(REACH - 1, at[REACH]).wait_recv()
        states = {s: partial(s, at[s]) for s in range(REACH, -1, -1)}
        for s in range(REACH, -1, -1):
            settle(s, at[s], states[s])
        return carry

    def ramp_down(i, carry):
        guarded(i, (), range(REACH - 1, -1, -1))
        return carry

    halves(0).wait_recv()
    lax.fori_loop(0, REACH, first, 0)
    halves(2).wait_recv()
    for h in range(OWN):
        vt[h] = vx[:, h * HD : (h + 1) * HD].astype(F32).T.astype(BF16)
    halves(1).wait_recv()
    halves(3).wait_recv()
    lax.fori_loop(REACH, SPAN, ramp_up, 0)
    lax.fori_loop(SPAN, CHUNKS + REACH * LAG, steady, 0)
    lax.fori_loop(CHUNKS + REACH * LAG, CHUNKS + SPAN, ramp_down, 0)

    theirs = fine.at[pl.ds(other * OWN, OWN), pl.ds(LEAD, ROWS), :]
    pltpu.make_async_copy(theirs, theirs, f_recv.at[0]).wait()

    @pl.when(core == 0)
    def _():
        rim = fine.at[:, pl.ds(8, 16), :]
        pltpu.make_async_copy(rim, rim, e_recv.at[0]).wait()

    @pl.when(core == 1)
    def _():
        rim = fine.at[pl.ds(0, OWN), pl.ds(8, 16), :]
        pltpu.make_async_copy(rim, rim, e_recv.at[0]).wait()

    square = jnp.zeros((16, 1), F32)
    for h in range(HEADS):
        at = slice(h * HD, (h + 1) * HD)
        fine[h, 0:8, :] = jnp.zeros((8, HD), F32)
        fine[h, 8:LEAD, :] = jnp.where(me > 0, fine[h, 8:LEAD, :], 0.0)
        row = jnp.zeros((68, HD), F32)
        for k in range(SHORT):
            row = row + fine[h, pl.ds(LEAD - 19 + k, 68, stride=SHORT), :] * pf_ref[k : k + 1, at]
        mid[h, 0:68, :] = rounded(row)
        row = jnp.zeros((16, HD), F32)
        for k in range(SHORT):
            row = row + mid[h, pl.ds(1 + k, 16, stride=SHORT), :] * pc_ref[k : k + 1, at]
        row = rounded(row)
        summit[:, at] = row
        square = square + jnp.sum(row * row, axis=1, keepdims=True)
    normed[...] = (summit[...] * lax.rsqrt(square / WIDTH + 1e-05) * ng_ref[...].reshape(1, WIDTH)).astype(BF16)

    def n_copy(step):
        target = (zc + step) % n_chip
        return remote(normed, na.at[sub], n_send.at[step], n_recv.at[sub], (ctx, 2 * target))

    def n_arrival(source):
        return remote(normed, na.at[source], n_send.at[0], n_recv.at[source], sibling)

    for step in range(1, n_chip):
        n_copy(step).start()

    @pl.when(core == 1)
    def _():
        n_copy(0).start()

    def spread(i):
        unit = 18 * zc + i
        piece = unit // 8
        head = piece % CHEADS
        at = pl.multiple_of((piece // CHEADS) * HD + (unit % 8) * UNIT, UNIT)
        src, dst = pt.at[pl.ds(i * UNIT, UNIT)], hb.at[pl.ds(at, UNIT)]
        return (
            head,
            lambda: remote(src, dst, u_send.at[i], u_recv.at[0], (ctx, 2 * head)),
            lambda: pltpu.make_async_copy(src, dst, u_recv.at[0]),
        )

    def k_copy(source, step):
        return remote(kb.at[source], kb.at[source], k_send.at[step], k_recv.at[source], (source + step, sub))

    def v_copy(source, step):
        return remote(vb.at[source], vb.at[source], v_send.at[step], v_recv.at[source], (source + step, sub))

    def a_copy(step):
        return remote(ah.at[zc], ah.at[zc], a_send.at[step], a_recv.at[zc], (ctx, 2 * ((zc + step) % n_chip)))

    def l_copy(step):
        target = (sub + step) % n_sub
        rows = pl.ds(pl.multiple_of(target * UNIT, UNIT), UNIT)
        return remote(ls.at[:, rows, :], lb.at[zc], l_send.at[step], l_recv.at[zc], (ctx, target))

    @pl.when(core == 0)
    def _():
        na[sub] = normed[...]
        for copy in weight_copies():
            copy.wait_recv()
        for source in range(n_sub):
            @pl.when(source != sub)
            def _(source=source):
                n_arrival(source).wait_recv()
        rows = na[...].reshape(ROWS, WIDTH)
        for turn, w in enumerate((wq_ref, wqs)):
            pt[turn * QKV_COLS : (turn + 1) * QKV_COLS, :] = nt(w[...], rows).astype(BF16)
        for i in range(18):
            head, away, here = spread(i)

            @pl.when(head == zc)
            def _(here=here):
                here().start()

            @pl.when(head != zc)
            def _(away=away):
                away().start()

    @pl.when((core == 0) & (zc < CHEADS))
    def _():
        pltpu.make_async_copy(hb, hb, u_recv.at[0]).wait()
        queries = hb[0:HD].astype(F32).T.astype(BF16)
        kb[ctx] = hb[HD : 2 * HD].astype(F32).T.astype(BF16)
        vb[ctx] = hb[2 * HD : 3 * HD]
        for step in range(1, n_ctx):
            @pl.when(ctx + step < n_ctx)
            def _(step=step):
                k_copy(ctx, step).start()
                v_copy(ctx, step).start()

        t = nt(kb[ctx], queries) * SCALE
        key_row = lax.broadcasted_iota(jnp.int32, t.shape, 0)
        query_row = lax.broadcasted_iota(jnp.int32, t.shape, 1)
        t = jnp.where(key_row <= query_row, t, NEG)
        peak = jnp.max(t, axis=0, keepdims=True)
        p = jnp.exp2(t - peak)
        total = jnp.sum(p, axis=0, keepdims=True)
        osc[...] = dot(vb[ctx], p.astype(BF16))

        def fold(i, carry):
            before, total = carry
            source = ctx - 1 - i
            k_copy(source, 1).wait_recv()
            v_copy(source, 1).wait_recv()
            t = nt(kb[source], queries) * SCALE
            peak = jnp.maximum(before, jnp.max(t, axis=0, keepdims=True))
            p = jnp.exp2(t - peak)
            a = jnp.exp2(before - peak)
            osc[...] = osc[...] * a + dot(vb[source], p.astype(BF16))
            return peak, total * a + jnp.sum(p, axis=0, keepdims=True)

        peak, total = lax.fori_loop(0, ctx, fold, (peak, total))
        ah[zc] = (osc[...] / total).T.astype(BF16)
        for step in range(1, n_chip):
            a_copy(step).start()

    @pl.when(core == 0)
    def _():
        for head in range(CHEADS):
            @pl.when(head != zc)
            def _(head=head):
                remote(ah.at[head], ah.at[head], a_send.at[0], a_recv.at[head], sibling).wait_recv()
        pad = jnp.zeros((ROWS, HD - OUT_COLS), F32)
        for turn, w in enumerate((wo_ref, wos)):
            lifted = nt(ah[0], w[:, 0:HD])
            for head in range(1, CHEADS):
                lifted = lifted + nt(ah[head], w[:, head * HD : (head + 1) * HD])
            ls[turn] = jnp.concatenate([lifted, pad], axis=1).astype(BF16)
        for step in range(1, n_sub):
            l_copy(step).start()
        lb[zc] = ls[:, pl.ds(pl.multiple_of(sub * UNIT, UNIT), UNIT), :]

    for source in range(n_chip):
        @pl.when((core == 1) | (source != zc))
        def _(source=source):
            remote(ls.at[:, 0:UNIT, :], lb.at[source], l_send.at[0], l_recv.at[source], sibling).wait_recv()

    pieces = []
    for source in range(n_chip):
        for turn in range(2):
            pieces.append(lb[source, turn].astype(F32)[:, :OUT_COLS])
    summit[...] = summit[...] + jnp.concatenate(pieces, axis=1)

    for h in range(HEADS):
        at = slice(h * HD, (h + 1) * HD)
        lift = summit[:, at]
        for k in range(SHORT):
            spots = pl.ds(4 + k, 16, stride=SHORT)
            mid[h, spots, :] = mid[h, spots, :] + uc_ref[k : k + 1, at] * lift
        lift = mid[h, 4:68, :]
        for k in range(SHORT):
            spots = pl.ds(LEAD + k, 64, stride=SHORT)
            fine[h, spots, :] = fine[h, spots, :] + uf_ref[k : k + 1, at] * lift
        out_ref[:, at] = fine[h, LEAD : LEAD + ROWS, :].astype(BF16)

    for n in range(4):
        halves(n).wait_send()
    for s in range(REACH):
        for slot in range(SLOTS):
            q_copy(s, CHUNKS - SLOTS + slot).wait_send()
            o_copy(s + 1, CHUNKS - SLOTS + slot).wait_send()
    for h in range(OWN):
        for half in range(2):
            f_copy(h, half).wait_send()
        edge_of(h, right_first, 1).wait_send()

        @pl.when(core == 0)
        def _(h=h):
            edge_of(h, twin, 0).wait_send()

    @pl.when(core == 1)
    def _():
        for copy in weight_copies():
            copy.wait_send()
        n_copy(0).wait_send()

    for step in range(1, n_chip):
        n_copy(step).wait_send()

    @pl.when(core == 0)
    def _():
        for i in range(18):
            head, away, here = spread(i)

            @pl.when(head != zc)
            def _(away=away):
                away().wait_send()
        for step in range(1, n_sub):
            l_copy(step).wait_send()

    @pl.when((core == 0) & (zc < CHEADS))
    def _():
        for step in range(1, n_ctx):
            @pl.when(ctx + step < n_ctx)
            def _(step=step):
                k_copy(ctx, step).wait_send()
                v_copy(ctx, step).wait_send()
        for step in range(1, n_chip):
            a_copy(step).wait_send()


def solution(mesh):
    n_ctx, n_sub = mesh.shape["ctx"], mesh.shape["sub"]
    n_chip = n_sub // 2
    dma = pltpu.SemaphoreType.DMA

    def shards(stream, q, k, v, pf, pc, uf, uc, ng, wq, wo):
        vmem = pl.BlockSpec(memory_space=pltpu.VMEM)
        return pl.pallas_call(
            functools.partial(kernel, n_ctx, n_sub),
            out_shape=jax.ShapeDtypeStruct((ROWS, WIDTH), BF16),
            in_specs=[vmem] * 11,
            out_specs=vmem,
            scratch_shapes=[
                *[pltpu.VMEM((CHIP_ROWS, OWN * HD), BF16)] * 4,
                pltpu.VMEM((REACH, CHUNKS, HALF, HD), BF16),
                pltpu.VMEM((REACH, CHUNKS, OROWS, HALF), BF16),
                pltpu.VMEM((REACH, SLOTS, OROWS, HALF), BF16),
                pltpu.VMEM((OWN, HD, CHIP_ROWS), BF16),
                pltpu.VMEM((OWN, 4, HALF, HD), F32),
                pltpu.VMEM((HEADS, LEAD + ROWS, HD), F32),
                pltpu.VMEM((HEADS, MROWS, HD), F32),
                pltpu.VMEM((16, WIDTH), F32),
                pltpu.VMEM((16, WIDTH), BF16),
                pltpu.VMEM((n_sub, 16, WIDTH), BF16),
                pltpu.VMEM((QKV_COLS, WIDTH), BF16),
                pltpu.VMEM((OUT_COLS, CHEADS * HD), BF16),
                pltpu.VMEM((2 * QKV_COLS, ROWS), BF16),
                pltpu.VMEM((3 * HD, ROWS), BF16),
                pltpu.VMEM((n_ctx, ROWS, HD), BF16),
                pltpu.VMEM((n_ctx, HD, ROWS), BF16),
                pltpu.VMEM((HD, ROWS), F32),
                pltpu.VMEM((CHEADS, ROWS, HD), BF16),
                pltpu.VMEM((2, ROWS, HD), BF16),
                pltpu.VMEM((n_chip, 2, UNIT, HD), BF16),
                dma((4,)), dma((4,)),
                dma((REACH, SLOTS)), dma((REACH, CHUNKS)),
                dma((REACH, SLOTS)), dma((REACH, CHUNKS)),
                dma((OWN, 2)), dma((1,)),
                dma((OWN, 2)), dma((1,)),
                dma((2,)), dma((2,)),
                dma((n_chip,)), dma((n_sub,)),
                dma((18,)), dma((1,)),
                dma((n_ctx,)), dma((n_ctx,)),
                dma((n_ctx,)), dma((n_ctx,)),
                dma((n_chip,)), dma((CHEADS,)),
                dma((n_sub,)), dma((n_chip,)),
            ],
            compiler_params=pltpu.CompilerParams(
                collective_id=0, has_side_effects=True, vmem_limit_bytes=60 * 2**20
            ),
        )(q, k, v, stream, pf, pc, uf, uc, ng, wq.T, wo.T)

    rows = P(("ctx", "sub"), None)
    return jax.shard_map(
        shards,
        mesh=mesh,
        in_specs=(rows, rows, rows, rows, P(), P(), P(), P(), P(), P(None, "sub"), P(None, "sub")),
        out_specs=rows,
        check_vma=False,
    )
```

time: 209 us -> 160 us (0.77)
  Pallas kernels: 201 us -> 158 us
  local copies, waits for them, and re-layouts: 7.24 us -> 2.06 us
    pallas_call x1, Pallas kernels: 201 us -> 158 us  [shards(): pl.pallas_call(functools.partial(kernel, n_ctx, n_sub), out_shape=jax.Sha...]
    unnamed x3 -> x1, local copies, waits for them, and re-layouts: 5.95 us -> 2.06 us
where the time goes in v2:
time: 160 us
  Pallas kernels  158 us (99%)
  local copies, waits for them, and re-layouts  2.06 us (1%)
    pallas_call x1, Pallas kernels, shards(): pl.pallas_call(functools.partial(kernel, n_ctx, n_sub), out_shape=jax.Sha...  158 us

profile of v2, /device:TPU:29, one launch (start us, length us, event | category | flops | bytes accessed | tf_op | source)
XLA Modules:
  0.0 159.6 jit_solution(7259720251762820150)
XLA Ops:
  0.0 157.5 %shard_map.109 = bf16[256,1536]{1,0:T(8,128)(2,1)} custom-call(bf16[256,1536]{1,0:T(8,128)(2,1)} %q_ref.1, bf16[256,1536]{1,0:T(8,128)(2,1)} %k_ref.1, bf16[256,1536]{1,0:T(8,128)(2,1)} %v_ref.1, bf16[256,1536]{1,0:T(8,128)(2,1)} %x_ref.1, f32[4,1536]{1,0:T(4,128)} %pf_ref.1, f32[4,1536]{1,0:T(4,128)} %pc_ref.1, f32[4,1536]{1,0:T(4,128)} %uf_ref.1, ...), custom_call_target="tpu_custom_call" | custom-call | tf_op jit(solution)/shard_map/pallas_call | solution.py:520
  157.5 2.1 %copy.13 = bf16[256,1536]{1,0:T(8,128)(2,1)} copy(bf16[256,1536]{1,0:T(8,128)(2,1)} %shard_map.109) | data formatting | bytes 1572864

commit v3 on v2

--- a/solution.py
+++ b/solution.py
@@ -23,8 +23,9 @@
 BLOCKS = CHIP_ROWS // HALF
 REACH = 3
 CHUNKS = OWN * BLOCKS
-LAG = 2
+LAG = 3
 SLOTS = 4
+POOLED = ((0, 3), (3, 2), (5, 1))
 SPAN = 2 * REACH * LAG
 WIDTH = HEADS * HD
 OROWS = HD + 16
@@ -53,10 +54,10 @@
     n_ctx, n_sub,
     q_ref, k_ref, v_ref, x_ref, pf_ref, pc_ref, uf_ref, uc_ref, ng_ref, wq_ref, wo_ref,
     out_ref,
-    qx, kx, vx, xx, qbuf, oin, oout, vt, fout, fine, mid, summit, normed, na, wqs, wos, pt, hb,
-    kb, vb, osc, ah, ls, lb,
-    x_send, x_recv, q_send, q_recv, o_send, o_recv, f_send, f_recv, e_send, e_recv, w_send, w_recv,
-    n_send, n_recv, u_send, u_recv, k_send, k_recv, v_send, v_recv, a_send, a_recv, l_send, l_recv,
+    qx, kx, vx, xx, qbuf, oin, oout, vt, fout, fine, mid, summit, pooled, na, wqs, pt, hb,
+    kb, vb, osc, att, ah, ls, lb, wof,
+    i_sem, x_send, x_recv, q_send, q_recv, o_send, o_recv, f_send, f_recv, e_send, e_recv, w_send, w_recv,
+    n_send, n_recv, u_send, u_recv, k_send, k_recv, v_send, v_recv, a_send, a_recv, l_send, l_recv, up_send, up_recv, down_send, down_recv,
 ):
     ctx = lax.axis_index("ctx")
     sub = lax.axis_index("sub")
@@ -97,35 +98,65 @@
     own_lanes = pl.ds(pl.multiple_of(core * OWN * HD, HD), OWN * HD)
     twin_lanes = pl.ds(pl.multiple_of(other * OWN * HD, HD), OWN * HD)
     parts = ((q_ref, qx), (k_ref, kx), (v_ref, vx), (x_ref, xx))
-    for src, dst in parts:
-        dst[own_rows, :] = src[:, own_lanes]
+
+    def inward(n):
+        src, dst = parts[n]
+        return pltpu.make_async_copy(src.at[:, own_lanes], dst.at[own_rows], i_sem.at[n])
+
+    for n in (2, 0, 1, 3):
+        inward(n).start()
+
+    def turned(rows):
+        for h in range(OWN):
+            vt[h, :, rows] = vx[rows, h * HD : (h + 1) * HD].astype(F32).T.astype(BF16)
+
+    inward(2).wait()
+    turned(own_rows)
+    inward(0).wait()
 
     def halves(n):
         src, dst = parts[n]
         return remote(src.at[:, twin_lanes], dst.at[own_rows], x_send.at[n], x_recv.at[n], twin)
 
     pl.semaphore_wait(barrier, 4 + (n_sub - 1) + (n_ctx - 1))
-    for n in range(4):
+    for n in (0, 2, 1, 3):
         halves(n).start()
 
     sibling = (ctx, 2 * zc)
 
-    def weight_copies():
-        return (
-            remote(wq_ref, wqs, w_send.at[0], w_recv.at[0], sibling),
-            remote(wo_ref, wos, w_send.at[1], w_recv.at[1], sibling),
-        )
+    def weight_copy():
+        return remote(wq_ref, wqs, w_send.at[0], w_recv.at[0], sibling)
 
     @pl.when(core == 1)
     def _():
-        for copy in weight_copies():
-            copy.start()
+        weight_copy().start()
+
+    def ring(hop, step, send, recv):
+        source = (zc - step * (hop - 1) + n_chip) % n_chip
+        src = wo_ref if hop == 1 else wof.at[source]
+        target = (zc + step + n_chip) % n_chip
+        return remote(src, wof.at[source], send.at[hop], recv.at[hop], (ctx, 2 * target + core))
+
+    def up(hop):
+        return ring(hop, 1, up_send, up_recv)
+
+    def down(hop):
+        return ring(hop, -1, down_send, down_recv)
+
+    def pass_on(way, hop):
+        if hop > 1:
+            way(hop - 1).wait_recv()
+        way(hop).start()
+
+    n_up, n_down = (n_chip - 1) // 2, n_chip // 2
+    wof[zc] = wo_ref[...]
+    pass_on(up, 1)
 
     def lanes(h):
         return pl.ds(pl.multiple_of(h * HD, HD), HD)
 
     def place(g):
-        return g // BLOCKS, (g + 2 * core) % BLOCKS
+        return g // BLOCKS, (g + BLOCKS - 1) % BLOCKS
 
     def block_rows(block):
         return pl.ds(pl.multiple_of(block * HALF, HALF), HALF)
@@ -147,13 +178,13 @@
     def f_copy(h, half):
         head = core * OWN + h
         rows = pl.ds(pl.multiple_of(LEAD + half * HALF, 8), HALF)
-        return remote(fout.at[h, half], fine.at[head, rows, :], f_send.at[h, half], f_recv.at[0], twin)
+        return remote(fout.at[h, half], fine.at[head, rows, :], f_send.at[h, half], f_recv.at[h], twin)
 
     def edge_of(h, device, slot):
         head = core * OWN + h
         return remote(
             fout.at[h, 2 + slot, pl.ds(HALF - 16, 16), :], fine.at[head, pl.ds(8, 16), :],
-            e_send.at[h, slot], e_recv.at[0], device,
+            e_send.at[h, slot], e_recv.at[h, core], device,
         )
 
     def forward(s, g):
@@ -261,6 +292,11 @@
         return carry
 
     def ramp_up(i, carry):
+        for hop in range(2, n_up + 1):
+            @pl.when(i == 4 * hop)
+            def _(hop=hop):
+                pass_on(up, hop)
+
         guarded(i, range(REACH), range(REACH, -1, -1))
         return carry
 
@@ -286,57 +322,81 @@
     halves(0).wait_recv()
     lax.fori_loop(0, REACH, first, 0)
     halves(2).wait_recv()
-    for h in range(OWN):
-        vt[h] = vx[:, h * HD : (h + 1) * HD].astype(F32).T.astype(BF16)
+    turned(pl.ds(pl.multiple_of(other * ROWS, ROWS), ROWS))
+    inward(1).wait()
+    inward(3).wait()
     halves(1).wait_recv()
     halves(3).wait_recv()
     lax.fori_loop(REACH, SPAN, ramp_up, 0)
     lax.fori_loop(SPAN, CHUNKS + REACH * LAG, steady, 0)
-    lax.fori_loop(CHUNKS + REACH * LAG, CHUNKS + SPAN, ramp_down, 0)
-
-    theirs = fine.at[pl.ds(other * OWN, OWN), pl.ds(LEAD, ROWS), :]
-    pltpu.make_async_copy(theirs, theirs, f_recv.at[0]).wait()
-
-    @pl.when(core == 0)
-    def _():
-        rim = fine.at[:, pl.ds(8, 16), :]
-        pltpu.make_async_copy(rim, rim, e_recv.at[0]).wait()
-
-    @pl.when(core == 1)
-    def _():
-        rim = fine.at[pl.ds(0, OWN), pl.ds(8, 16), :]
-        pltpu.make_async_copy(rim, rim, e_recv.at[0]).wait()
-
-    square = jnp.zeros((16, 1), F32)
-    for h in range(HEADS):
-        at = slice(h * HD, (h + 1) * HD)
-        fine[h, 0:8, :] = jnp.zeros((8, HD), F32)
-        fine[h, 8:LEAD, :] = jnp.where(me > 0, fine[h, 8:LEAD, :], 0.0)
-        row = jnp.zeros((68, HD), F32)
-        for k in range(SHORT):
-            row = row + fine[h, pl.ds(LEAD - 19 + k, 68, stride=SHORT), :] * pf_ref[k : k + 1, at]
-        mid[h, 0:68, :] = rounded(row)
-        row = jnp.zeros((16, HD), F32)
-        for k in range(SHORT):
-            row = row + mid[h, pl.ds(1 + k, 16, stride=SHORT), :] * pc_ref[k : k + 1, at]
-        row = rounded(row)
-        summit[:, at] = row
-        square = square + jnp.sum(row * row, axis=1, keepdims=True)
-    normed[...] = (summit[...] * lax.rsqrt(square / WIDTH + 1e-05) * ng_ref[...].reshape(1, WIDTH)).astype(BF16)
-
-    def n_copy(step):
+
+    def edge_arrival(h, side):
+        head = side * OWN + h
+        rim = fine.at[head, pl.ds(8, 16), :]
+        pltpu.make_async_copy(rim, rim, e_recv.at[h, side]).wait()
+
+    def pool(h):
+        theirs = fine.at[other * OWN + h, pl.ds(LEAD, ROWS), :]
+        pltpu.make_async_copy(theirs, theirs, f_recv.at[h]).wait()
+        edge_arrival(h, 0)
+
+        @pl.when(core == 0)
+        def _():
+            edge_arrival(h, 1)
+
+        for side in range(2):
+            head = side * OWN + h
+            at = slice(head * HD, (head + 1) * HD)
+            fine[head, 0:8, :] = jnp.zeros((8, HD), F32)
+            fine[head, 8:LEAD, :] = jnp.where(me > 0, fine[head, 8:LEAD, :], 0.0)
+            row = jnp.zeros((68, HD), F32)
+            for k in range(SHORT):
+                row = row + fine[head, pl.ds(LEAD - 19 + k, 68, stride=SHORT), :] * pf_ref[k : k + 1, at]
+            mid[head, 0:68, :] = rounded(row)
+            row = jnp.zeros((16, HD), F32)
+            for k in range(SHORT):
+                row = row + mid[head, pl.ds(1 + k, 16, stride=SHORT), :] * pc_ref[k : k + 1, at]
+            row = row.astype(BF16)
+            summit[:, at] = row.astype(F32)
+            pooled[h, :, side * HD : (side + 1) * HD] = row
+
+    def n_copy(batch, step):
+        first, count = POOLED[batch]
         target = (zc + step) % n_chip
-        return remote(normed, na.at[sub], n_send.at[step], n_recv.at[sub], (ctx, 2 * target))
-
-    def n_arrival(source):
-        return remote(normed, na.at[source], n_send.at[0], n_recv.at[source], sibling)
-
-    for step in range(1, n_chip):
-        n_copy(step).start()
-
-    @pl.when(core == 1)
-    def _():
-        n_copy(0).start()
+        span = pl.ds(first, count)
+        return remote(
+            pooled.at[span], na.at[sub, span], n_send.at[batch, step], n_recv.at[batch, sub], (ctx, 2 * target)
+        )
+
+    def n_arrival(batch, source):
+        first, count = POOLED[batch]
+        span = pl.ds(first, count)
+        return remote(
+            pooled.at[span], na.at[source, span], n_send.at[batch, 0], n_recv.at[batch, source], sibling
+        )
+
+    def share(batch):
+        first, count = POOLED[batch]
+        for h in range(first, first + count):
+            pool(h)
+        for step in range(1, n_chip):
+            n_copy(batch, step).start()
+
+        @pl.when(core == 1)
+        def _():
+            n_copy(batch, 0).start()
+
+        @pl.when(core == 0)
+        def _():
+            na[sub, first : first + count] = pooled[first : first + count]
+
+    share(0)
+    pass_on(down, 1)
+    lax.fori_loop(CHUNKS + REACH * LAG, CHUNKS + SPAN - 2, ramp_down, 0)
+    share(1)
+    pass_on(down, 2)
+    lax.fori_loop(CHUNKS + SPAN - 2, CHUNKS + SPAN, ramp_down, 0)
+    share(2)
 
     def spread(i):
         unit = 18 * zc + i
@@ -357,25 +417,37 @@
         return remote(vb.at[source], vb.at[source], v_send.at[step], v_recv.at[source], (source + step, sub))
 
     def a_copy(step):
-        return remote(ah.at[zc], ah.at[zc], a_send.at[step], a_recv.at[zc], (ctx, 2 * ((zc + step) % n_chip)))
-
-    def l_copy(step):
         target = (sub + step) % n_sub
-        rows = pl.ds(pl.multiple_of(target * UNIT, UNIT), UNIT)
-        return remote(ls.at[:, rows, :], lb.at[zc], l_send.at[step], l_recv.at[zc], (ctx, target))
+        rows = pl.ds(pl.multiple_of((target // 2) * 2 * UNIT, 2 * UNIT), 2 * UNIT)
+        return remote(att.at[rows], ah.at[zc], a_send.at[step], a_recv.at[zc], (ctx, target))
 
     @pl.when(core == 0)
     def _():
-        na[sub] = normed[...]
-        for copy in weight_copies():
-            copy.wait_recv()
-        for source in range(n_sub):
-            @pl.when(source != sub)
-            def _(source=source):
-                n_arrival(source).wait_recv()
-        rows = na[...].reshape(ROWS, WIDTH)
-        for turn, w in enumerate((wq_ref, wqs)):
-            pt[turn * QKV_COLS : (turn + 1) * QKV_COLS, :] = nt(w[...], rows).astype(BF16)
+        weight_copy().wait_recv()
+        for batch in range(len(POOLED)):
+            for source in range(n_sub):
+                @pl.when(source != sub)
+                def _(batch=batch, source=source):
+                    n_arrival(batch, source).wait_recv()
+
+        def wide(h):
+            return na[:, h].reshape(ROWS, 2 * HD).astype(F32)
+
+        def pair(ref, h):
+            head = OWN + h
+            return jnp.concatenate([ref[:, h * HD : (h + 1) * HD], ref[:, head * HD : (head + 1) * HD]], axis=1)
+
+        gain = ng_ref[...].reshape(1, WIDTH)
+        square = jnp.zeros((ROWS, 1), F32)
+        for h in range(OWN):
+            square = square + jnp.sum(wide(h) * wide(h), axis=1, keepdims=True)
+        scale = lax.rsqrt(square / WIDTH + 1e-05)
+        sums = [jnp.zeros((QKV_COLS, ROWS), F32)] * 2
+        for h in range(OWN):
+            rows = (wide(h) * scale * pair(gain, h)).astype(BF16)
+            sums = [total + nt(pair(w, h), rows) for total, w in zip(sums, (wq_ref, wqs))]
+        for turn in range(2):
+            pt[turn * QKV_COLS : (turn + 1) * QKV_COLS, :] = sums[turn].astype(BF16)
         for i in range(18):
             head, away, here = spread(i)
 
@@ -387,10 +459,11 @@
             def _(away=away):
                 away().start()
 
+    pass_on(down, 3)
+
     @pl.when((core == 0) & (zc < CHEADS))
     def _():
         pltpu.make_async_copy(hb, hb, u_recv.at[0]).wait()
-        queries = hb[0:HD].astype(F32).T.astype(BF16)
         kb[ctx] = hb[HD : 2 * HD].astype(F32).T.astype(BF16)
         vb[ctx] = hb[2 * HD : 3 * HD]
         for step in range(1, n_ctx):
@@ -399,6 +472,12 @@
                 k_copy(ctx, step).start()
                 v_copy(ctx, step).start()
 
+    for hop in range(4, n_down + 1):
+        pass_on(down, hop)
+
+    @pl.when((core == 0) & (zc < CHEADS))
+    def _():
+        queries = hb[0:HD].astype(F32).T.astype(BF16)
         t = nt(kb[ctx], queries) * SCALE
         key_row = lax.broadcasted_iota(jnp.int32, t.shape, 0)
         query_row = lax.broadcasted_iota(jnp.int32, t.shape, 1)
@@ -421,35 +500,39 @@
             return peak, total * a + jnp.sum(p, axis=0, keepdims=True)
 
         peak, total = lax.fori_loop(0, ctx, fold, (peak, total))
-        ah[zc] = (osc[...] / total).T.astype(BF16)
-        for step in range(1, n_chip):
+        att[...] = (osc[...] / total).T.astype(BF16)
+        for step in range(1, n_sub):
             a_copy(step).start()
-
-    @pl.when(core == 0)
-    def _():
-        for head in range(CHEADS):
-            @pl.when(head != zc)
-            def _(head=head):
-                remote(ah.at[head], ah.at[head], a_send.at[0], a_recv.at[head], sibling).wait_recv()
-        pad = jnp.zeros((ROWS, HD - OUT_COLS), F32)
-        for turn, w in enumerate((wo_ref, wos)):
-            lifted = nt(ah[0], w[:, 0:HD])
-            for head in range(1, CHEADS):
-                lifted = lifted + nt(ah[head], w[:, head * HD : (head + 1) * HD])
-            ls[turn] = jnp.concatenate([lifted, pad], axis=1).astype(BF16)
-        for step in range(1, n_sub):
-            l_copy(step).start()
-        lb[zc] = ls[:, pl.ds(pl.multiple_of(sub * UNIT, UNIT), UNIT), :]
-
+        ah[zc] = att[pl.ds(pl.multiple_of(zc * 2 * UNIT, 2 * UNIT), 2 * UNIT), :]
+
+    up(n_up).wait_recv()
+    down(n_down).wait_recv()
+    for head in range(CHEADS):
+        @pl.when((core == 1) | (head != zc))
+        def _(head=head):
+            remote(att.at[0 : 2 * UNIT], ah.at[head], a_send.at[0], a_recv.at[head], sibling).wait_recv()
+    rows = jnp.concatenate([ah[head] for head in range(CHEADS)], axis=1)
+    pad = jnp.zeros((2 * UNIT, HD - OUT_COLS), F32)
     for source in range(n_chip):
-        @pl.when((core == 1) | (source != zc))
-        def _(source=source):
-            remote(ls.at[:, 0:UNIT, :], lb.at[source], l_send.at[0], l_recv.at[source], sibling).wait_recv()
-
+        lifted = jnp.concatenate([nt(rows, wof[source]), pad], axis=1).astype(BF16)
+
+        @pl.when(core == 0)
+        def _(lifted=lifted, source=source):
+            lb[0, source] = lifted[:UNIT]
+            ls[source] = lifted[UNIT:]
+
+        @pl.when(core == 1)
+        def _(lifted=lifted, source=source):
+            lb[1, source] = lifted[UNIT:]
+            ls[source] = lifted[:UNIT]
+
+    l_copy = remote(ls, lb.at[core], l_send.at[0], l_recv.at[0], twin)
+    l_copy.start()
+    remote(ls, lb.at[other], l_send.at[0], l_recv.at[0], twin).wait_recv()
     pieces = []
     for source in range(n_chip):
         for turn in range(2):
-            pieces.append(lb[source, turn].astype(F32)[:, :OUT_COLS])
+            pieces.append(lb[turn, source].astype(F32)[:, :OUT_COLS])
     summit[...] = summit[...] + jnp.concatenate(pieces, axis=1)
 
     for h in range(HEADS):
@@ -481,12 +564,18 @@
 
     @pl.when(core == 1)
     def _():
-        for copy in weight_copies():
-            copy.wait_send()
-        n_copy(0).wait_send()
-
-    for step in range(1, n_chip):
-        n_copy(step).wait_send()
+        weight_copy().wait_send()
+        for batch in range(len(POOLED)):
+            n_copy(batch, 0).wait_send()
+
+    for batch in range(len(POOLED)):
+        for step in range(1, n_chip):
+            n_copy(batch, step).wait_send()
+    for hop in range(1, n_up + 1):
+        up(hop).wait_send()
+    for hop in range(1, n_down + 1):
+        down(hop).wait_send()
+    l_copy.wait_send()
 
     @pl.when(core == 0)
     def _():
@@ -496,8 +585,6 @@
             @pl.when(head != zc)
             def _(away=away):
                 away().wait_send()
-        for step in range(1, n_sub):
-            l_copy(step).wait_send()
 
     @pl.when((core == 0) & (zc < CHEADS))
     def _():
@@ -506,7 +593,7 @@
             def _(step=step):
                 k_copy(ctx, step).wait_send()
                 v_copy(ctx, step).wait_send()
-        for step in range(1, n_chip):
+        for step in range(1, n_sub):
             a_copy(step).wait_send()
 
 
@@ -520,7 +607,7 @@
         return pl.pallas_call(
             functools.partial(kernel, n_ctx, n_sub),
             out_shape=jax.ShapeDtypeStruct((ROWS, WIDTH), BF16),
-            in_specs=[vmem] * 11,
+            in_specs=[pl.BlockSpec(memory_space=pl.ANY)] * 4 + [vmem] * 7,
             out_specs=vmem,
             scratch_shapes=[
                 *[pltpu.VMEM((CHIP_ROWS, OWN * HD), BF16)] * 4,
@@ -532,30 +619,33 @@
                 pltpu.VMEM((HEADS, LEAD + ROWS, HD), F32),
                 pltpu.VMEM((HEADS, MROWS, HD), F32),
                 pltpu.VMEM((16, WIDTH), F32),
-                pltpu.VMEM((16, WIDTH), BF16),
-                pltpu.VMEM((n_sub, 16, WIDTH), BF16),
+                pltpu.VMEM((OWN, 16, 2 * HD), BF16),
+                pltpu.VMEM((n_sub, OWN, 16, 2 * HD), BF16),
                 pltpu.VMEM((QKV_COLS, WIDTH), BF16),
-                pltpu.VMEM((OUT_COLS, CHEADS * HD), BF16),
                 pltpu.VMEM((2 * QKV_COLS, ROWS), BF16),
                 pltpu.VMEM((3 * HD, ROWS), BF16),
                 pltpu.VMEM((n_ctx, ROWS, HD), BF16),
                 pltpu.VMEM((n_ctx, HD, ROWS), BF16),
                 pltpu.VMEM((HD, ROWS), F32),
-                pltpu.VMEM((CHEADS, ROWS, HD), BF16),
-                pltpu.VMEM((2, ROWS, HD), BF16),
-                pltpu.VMEM((n_chip, 2, UNIT, HD), BF16),
-                dma((4,)), dma((4,)),
+                pltpu.VMEM((ROWS, HD), BF16),
+                pltpu.VMEM((CHEADS, 2 * UNIT, HD), BF16),
+                pltpu.VMEM((n_chip, UNIT, HD), BF16),
+                pltpu.VMEM((2, n_chip, UNIT, HD), BF16),
+                pltpu.VMEM((n_chip, OUT_COLS, CHEADS * HD), BF16),
+                dma((4,)), dma((4,)), dma((4,)),
                 dma((REACH, SLOTS)), dma((REACH, CHUNKS)),
                 dma((REACH, SLOTS)), dma((REACH, CHUNKS)),
-                dma((OWN, 2)), dma((1,)),
-                dma((OWN, 2)), dma((1,)),
-                dma((2,)), dma((2,)),
-                dma((n_chip,)), dma((n_sub,)),
+                dma((OWN, 2)), dma((OWN,)),
+                dma((OWN, 2)), dma((OWN, 2)),
+                dma((1,)), dma((1,)),
+                dma((len(POOLED), n_chip)), dma((len(POOLED), n_sub)),
                 dma((18,)), dma((1,)),
                 dma((n_ctx,)), dma((n_ctx,)),
                 dma((n_ctx,)), dma((n_ctx,)),
-                dma((n_chip,)), dma((CHEADS,)),
-                dma((n_sub,)), dma((n_chip,)),
+                dma((n_sub,)), dma((CHEADS,)),
+                dma((1,)), dma((1,)),
+                dma((n_chip,)), dma((n_chip,)),
+                dma((n_chip,)), dma((n_chip,)),
             ],
             compiler_params=pltpu.CompilerParams(
                 collective_id=0, has_side_effects=True, vmem_limit_bytes=60 * 2**20

time: 160 us -> 143 us (0.89)
  Pallas kernels: 158 us -> 141 us
    pallas_call x1, Pallas kernels: 158 us -> 141 us  [shards(): pl.pallas_call(functools.partial(kernel, n_ctx, n_sub), out_shape=jax.Sha...]
where the time goes in v3:
time: 143 us
  Pallas kernels  141 us (99%)
  local copies, waits for them, and re-layouts  2.06 us (1%)
    pallas_call x1, Pallas kernels, shards(): pl.pallas_call(functools.partial(kernel, n_ctx, n_sub), out_shape=jax.Sha...  141 us

profile of v3, /device:TPU:29, one launch (start us, length us, event | category | flops | bytes accessed | tf_op | source)
XLA Modules:
  0.0 143.3 jit_solution(3591818761081548152)
XLA Ops:
  0.0 141.3 %shard_map.109 = bf16[256,1536]{1,0:T(8,128)(2,1)} custom-call(bf16[256,1536]{1,0:T(8,128)(2,1)} %q_ref.1, bf16[256,1536]{1,0:T(8,128)(2,1)} %k_ref.1, bf16[256,1536]{1,0:T(8,128)(2,1)} %v_ref.1, bf16[256,1536]{1,0:T(8,128)(2,1)} %x_ref.1, f32[4,1536]{1,0:T(4,128)} %pf_ref.1, f32[4,1536]{1,0:T(4,128)} %pc_ref.1, f32[4,1536]{1,0:T(4,128)} %uf_ref.1, ...), custom_call_target="tpu_custom_call" | custom-call | tf_op jit(solution)/shard_map/pallas_call | solution.py:607
  141.3 2.1 %copy.13 = bf16[256,1536]{1,0:T(8,128)(2,1)} copy(bf16[256,1536]{1,0:T(8,128)(2,1)} %shard_map.109) | data formatting | bytes 1572864

commit v4 on v3

--- a/solution.py
+++ b/solution.py
@@ -28,7 +28,6 @@
 POOLED = ((0, 3), (3, 2), (5, 1))
 SPAN = 2 * REACH * LAG
 WIDTH = HEADS * HD
-OROWS = HD + 16
 LEAD = 24
 MROWS = 72
 QKV_COLS = 144
@@ -54,9 +53,9 @@
     n_ctx, n_sub,
     q_ref, k_ref, v_ref, x_ref, pf_ref, pc_ref, uf_ref, uc_ref, ng_ref, wq_ref, wo_ref,
     out_ref,
-    qx, kx, vx, xx, qbuf, oin, oout, vt, fout, fine, mid, summit, pooled, na, wqs, pt, hb,
+    qx, kx, vx, xx, qbuf, oin, oout, sin, sout, vt, fout, fine, mid, summit, pooled, na, wqs, pt, hb,
     kb, vb, osc, att, ah, ls, lb, wof,
-    i_sem, x_send, x_recv, q_send, q_recv, o_send, o_recv, f_send, f_recv, e_send, e_recv, w_send, w_recv,
+    i_sem, x_send, x_recv, q_send, q_recv, o_send, o_recv, s_send, s_recv, f_send, f_recv, e_send, e_recv, w_send, w_recv,
     n_send, n_recv, u_send, u_recv, k_send, k_recv, v_send, v_recv, a_send, a_recv, l_send, l_recv, up_send, up_recv, down_send, down_recv,
 ):
     ctx = lax.axis_index("ctx")
@@ -80,13 +79,13 @@
     def greet(device):
         pl.semaphore_signal(barrier, inc=1, device_id=device, device_id_type=MESH)
 
+    for step in range(n_ctx - 1, 0, -1):
+        greet(((ctx + step) % n_ctx, sub))
+    for step in range(1, n_sub):
+        greet((ctx, (sub + step) % n_sub))
     for near in (left, right):
         for side in range(2):
             greet((near // n_chip, 2 * (near % n_chip) + side))
-    for step in range(1, n_sub):
-        greet((ctx, (sub + step) % n_sub))
-    for step in range(1, n_ctx):
-        greet(((ctx + step) % n_ctx, sub))
 
     def remote(src, dst, send, recv, device):
         return pltpu.make_async_remote_copy(
@@ -156,7 +155,9 @@
         return pl.ds(pl.multiple_of(h * HD, HD), HD)
 
     def place(g):
-        return g // BLOCKS, (g + BLOCKS - 1) % BLOCKS
+        turn = g % BLOCKS
+        near = turn + 1 - 2 * (turn % 2)
+        return g // BLOCKS, near + core * (BLOCKS - 1 - turn - near)
 
     def block_rows(block):
         return pl.ds(pl.multiple_of(block * HALF, HALF), HALF)
@@ -173,6 +174,12 @@
         return remote(
             oout.at[s - 1, g % SLOTS], oin.at[s - 1, g], o_send.at[s - 1, g % SLOTS],
             o_recv.at[s - 1, g], right_id,
+        )
+
+    def s_copy(s, g):
+        return remote(
+            sout.at[s - 1, g % SLOTS], sin.at[s - 1, g], s_send.at[s - 1, g % SLOTS],
+            s_recv.at[s - 1, g], right_id,
         )
 
     def f_copy(h, half):
@@ -206,7 +213,7 @@
             key_row = lax.broadcasted_iota(jnp.int32, t.shape, 0)
             query_row = lax.broadcasted_iota(jnp.int32, t.shape, 1) + block * HALF
             t = jnp.where(key_row <= query_row if s == 0 else key_row > query_row, t, NEG)
-        peak = rounded(jnp.max(t, axis=0, keepdims=True))
+        peak = jnp.max(t, axis=0, keepdims=True)
         p = jnp.exp2(t - peak)
         total = jnp.sum(p, axis=0, keepdims=True)
         summed = dot(vt[h], p.astype(BF16))
@@ -218,14 +225,14 @@
         h, block = place(g)
         peak, total, summed = state
         if s < REACH:
-            o_copy(s + 1, g).wait_recv()
-            stats = oin[s, g, HD:OROWS, :].astype(F32)
-            before = stats[0:1]
+            s_copy(s + 1, g).wait_recv()
+            before = sin[s, g, 0:1, :]
             top = jnp.maximum(before, peak)
             a = jnp.exp2(before - top)
             b = jnp.exp2(peak - top)
-            summed = oin[s, g, 0:HD, :].astype(F32) * a + summed * b
-            total = (stats[1:2] + stats[2:3]) * a + total * b
+            total = sin[s, g, 1:2, :] * a + total * b
+            o_copy(s + 1, g).wait_recv()
+            summed = oin[s, g].astype(F32) * a + summed * b
             peak = top
         if s > 0:
             slot = g % SLOTS
@@ -233,12 +240,12 @@
             @pl.when(g >= SLOTS)
             def _():
                 o_copy(s, g - SLOTS).wait_send()
-
-            oout[s - 1, slot, 0:HD, :] = summed.astype(BF16)
-            high = rounded(total)
-            row = lax.broadcasted_iota(jnp.int32, (16, HALF), 0)
-            stats = jnp.where(row == 0, peak, jnp.where(row == 1, high, total - high))
-            oout[s - 1, slot, HD:OROWS, :] = stats.astype(BF16)
+                s_copy(s, g - SLOTS).wait_send()
+
+            sout[s - 1, slot, 0:1, :] = peak
+            sout[s - 1, slot, 1:2, :] = total
+            s_copy(s, g).start()
+            oout[s - 1, slot] = summed.astype(BF16)
             o_copy(s, g).start()
         else:
             attended = (summed / total).T
@@ -288,7 +295,7 @@
                 settle(s, g, partial(s, g))
 
     def first(i, carry):
-        guarded(i, range(REACH), ())
+        guarded(jnp.int32(i), range(REACH), ())
         return carry
 
     def ramp_up(i, carry):
@@ -319,8 +326,10 @@
         guarded(i, (), range(REACH - 1, -1, -1))
         return carry
 
+    first(0, 0)
+    first(1, 0)
     halves(0).wait_recv()
-    lax.fori_loop(0, REACH, first, 0)
+    first(2, 0)
     halves(2).wait_recv()
     turned(pl.ds(pl.multiple_of(other * ROWS, ROWS), ROWS))
     inward(1).wait()
@@ -424,23 +433,22 @@
     @pl.when(core == 0)
     def _():
         weight_copy().wait_recv()
-        for batch in range(len(POOLED)):
+        def wide(h):
+            return na[:, h].reshape(ROWS, 2 * HD).astype(F32)
+
+        def pair(ref, h):
+            head = OWN + h
+            return jnp.concatenate([ref[:, h * HD : (h + 1) * HD], ref[:, head * HD : (head + 1) * HD]], axis=1)
+
+        gain = ng_ref[...].reshape(1, WIDTH)
+        square = jnp.zeros((ROWS, 1), F32)
+        for batch, (start, count) in enumerate(POOLED):
             for source in range(n_sub):
                 @pl.when(source != sub)
                 def _(batch=batch, source=source):
                     n_arrival(batch, source).wait_recv()
-
-        def wide(h):
-            return na[:, h].reshape(ROWS, 2 * HD).astype(F32)
-
-        def pair(ref, h):
-            head = OWN + h
-            return jnp.concatenate([ref[:, h * HD : (h + 1) * HD], ref[:, head * HD : (head + 1) * HD]], axis=1)
-
-        gain = ng_ref[...].reshape(1, WIDTH)
-        square = jnp.zeros((ROWS, 1), F32)
-        for h in range(OWN):
-            square = square + jnp.sum(wide(h) * wide(h), axis=1, keepdims=True)
+            for h in range(start, start + count):
+                square = square + jnp.sum(wide(h) * wide(h), axis=1, keepdims=True)
         scale = lax.rsqrt(square / WIDTH + 1e-05)
         sums = [jnp.zeros((QKV_COLS, ROWS), F32)] * 2
         for h in range(OWN):
@@ -474,6 +482,17 @@
 
     for hop in range(4, n_down + 1):
         pass_on(down, hop)
+
+    for h in range(HEADS):
+        at = slice(h * HD, (h + 1) * HD)
+        row = summit[:, at]
+        for k in range(SHORT):
+            spots = pl.ds(4 + k, 16, stride=SHORT)
+            mid[h, spots, :] = mid[h, spots, :] + uc_ref[k : k + 1, at] * row
+        row = mid[h, 4:68, :]
+        for k in range(SHORT):
+            spots = pl.ds(LEAD + k, 64, stride=SHORT)
+            fine[h, spots, :] = fine[h, spots, :] + uf_ref[k : k + 1, at] * row
 
     @pl.when((core == 0) & (zc < CHEADS))
     def _():
@@ -512,40 +531,36 @@
         def _(head=head):
             remote(att.at[0 : 2 * UNIT], ah.at[head], a_send.at[0], a_recv.at[head], sibling).wait_recv()
     rows = jnp.concatenate([ah[head] for head in range(CHEADS)], axis=1)
-    pad = jnp.zeros((2 * UNIT, HD - OUT_COLS), F32)
-    for source in range(n_chip):
-        lifted = jnp.concatenate([nt(rows, wof[source]), pad], axis=1).astype(BF16)
-
-        @pl.when(core == 0)
-        def _(lifted=lifted, source=source):
-            lb[0, source] = lifted[:UNIT]
-            ls[source] = lifted[UNIT:]
-
-        @pl.when(core == 1)
-        def _(lifted=lifted, source=source):
-            lb[1, source] = lifted[UNIT:]
-            ls[source] = lifted[:UNIT]
+    both = nt(rows, wof[...].reshape(n_chip * OUT_COLS, CHEADS * HD)).astype(BF16)
+
+    @pl.when(core == 0)
+    def _():
+        lb[0] = both[:UNIT]
+        ls[...] = both[UNIT:]
+
+    @pl.when(core == 1)
+    def _():
+        lb[1] = both[UNIT:]
+        ls[...] = both[:UNIT]
 
     l_copy = remote(ls, lb.at[core], l_send.at[0], l_recv.at[0], twin)
     l_copy.start()
     remote(ls, lb.at[other], l_send.at[0], l_recv.at[0], twin).wait_recv()
+    sides = [lb[side].astype(F32) for side in range(2)]
     pieces = []
     for source in range(n_chip):
-        for turn in range(2):
-            pieces.append(lb[turn, source].astype(F32)[:, :OUT_COLS])
-    summit[...] = summit[...] + jnp.concatenate(pieces, axis=1)
+        for side in range(2):
+            pieces.append(sides[side][:, source * OUT_COLS : (source + 1) * OUT_COLS])
+    lifted = jnp.concatenate(pieces, axis=1)
 
     for h in range(HEADS):
         at = slice(h * HD, (h + 1) * HD)
-        lift = summit[:, at]
-        for k in range(SHORT):
-            spots = pl.ds(4 + k, 16, stride=SHORT)
-            mid[h, spots, :] = mid[h, spots, :] + uc_ref[k : k + 1, at] * lift
-        lift = mid[h, 4:68, :]
-        for k in range(SHORT):
-            spots = pl.ds(LEAD + k, 64, stride=SHORT)
-            fine[h, spots, :] = fine[h, spots, :] + uf_ref[k : k + 1, at] * lift
-        out_ref[:, at] = fine[h, LEAD : LEAD + ROWS, :].astype(BF16)
+        up_rows = [uc_ref[j : j + 1, at] * uf_ref[:, at] for j in range(SHORT)]
+        factor = jnp.concatenate(up_rows, axis=0)
+        for r in range(UNIT):
+            rows = slice(r * 16, (r + 1) * 16)
+            base = fine[h, LEAD + r * 16 : LEAD + (r + 1) * 16, :]
+            out_ref[rows, at] = (base + factor * lifted[r : r + 1, at]).astype(BF16)
 
     for n in range(4):
         halves(n).wait_send()
@@ -553,6 +568,7 @@
         for slot in range(SLOTS):
             q_copy(s, CHUNKS - SLOTS + slot).wait_send()
             o_copy(s + 1, CHUNKS - SLOTS + slot).wait_send()
+            s_copy(s + 1, CHUNKS - SLOTS + slot).wait_send()
     for h in range(OWN):
         for half in range(2):
             f_copy(h, half).wait_send()
@@ -612,8 +628,10 @@
             scratch_shapes=[
                 *[pltpu.VMEM((CHIP_ROWS, OWN * HD), BF16)] * 4,
                 pltpu.VMEM((REACH, CHUNKS, HALF, HD), BF16),
-                pltpu.VMEM((REACH, CHUNKS, OROWS, HALF), BF16),
-                pltpu.VMEM((REACH, SLOTS, OROWS, HALF), BF16),
+                pltpu.VMEM((REACH, CHUNKS, HD, HALF), BF16),
+                pltpu.VMEM((REACH, SLOTS, HD, HALF), BF16),
+                pltpu.VMEM((REACH, CHUNKS, 2, HALF), F32),
+                pltpu.VMEM((REACH, SLOTS, 2, HALF), F32),
                 pltpu.VMEM((OWN, HD, CHIP_ROWS), BF16),
                 pltpu.VMEM((OWN, 4, HALF, HD), F32),
                 pltpu.VMEM((HEADS, LEAD + ROWS, HD), F32),
@@ -629,10 +647,11 @@
                 pltpu.VMEM((HD, ROWS), F32),
                 pltpu.VMEM((ROWS, HD), BF16),
                 pltpu.VMEM((CHEADS, 2 * UNIT, HD), BF16),
-                pltpu.VMEM((n_chip, UNIT, HD), BF16),
-                pltpu.VMEM((2, n_chip, UNIT, HD), BF16),
+                pltpu.VMEM((UNIT, n_chip * OUT_COLS), BF16),
+                pltpu.VMEM((2, UNIT, n_chip * OUT_COLS), BF16),
                 pltpu.VMEM((n_chip, OUT_COLS, CHEADS * HD), BF16),
                 dma((4,)), dma((4,)), dma((4,)),
+                dma((REACH, SLOTS)), dma((REACH, CHUNKS)),
                 dma((REACH, SLOTS)), dma((REACH, CHUNKS)),
                 dma((REACH, SLOTS)), dma((REACH, CHUNKS)),
                 dma((OWN, 2)), dma((OWN,)),

time: 143 us -> 140 us (0.979)
  Pallas kernels: 141 us -> 138 us
    pallas_call x1, Pallas kernels: 141 us -> 138 us  [shards(): pl.pallas_call(functools.partial(kernel, n_ctx, n_sub), out_shape=jax.Sha...]
where the time goes in v4:
time: 140 us
  Pallas kernels  138 us (99%)
  local copies, waits for them, and re-layouts  2.06 us (1%)
    pallas_call x1, Pallas kernels, shards(): pl.pallas_call(functools.partial(kernel, n_ctx, n_sub), out_shape=jax.Sha...  138 us

profile of v4, /device:TPU:29, one launch (start us, length us, event | category | flops | bytes accessed | tf_op | source)
XLA Modules:
  0.0 139.9 jit_solution(2360080342256889346)
XLA Ops:
  0.0 137.8 %shard_map.109 = bf16[256,1536]{1,0:T(8,128)(2,1)} custom-call(bf16[256,1536]{1,0:T(8,128)(2,1)} %q_ref.1, bf16[256,1536]{1,0:T(8,128)(2,1)} %k_ref.1, bf16[256,1536]{1,0:T(8,128)(2,1)} %v_ref.1, bf16[256,1536]{1,0:T(8,128)(2,1)} %x_ref.1, f32[4,1536]{1,0:T(4,128)} %pf_ref.1, f32[4,1536]{1,0:T(4,128)} %pc_ref.1, f32[4,1536]{1,0:T(4,128)} %uf_ref.1, ...), custom_call_target="tpu_custom_call" | custom-call | tf_op jit(solution)/shard_map/pallas_call | solution.py:623
  137.8 2.1 %copy.13 = bf16[256,1536]{1,0:T(8,128)(2,1)} copy(bf16[256,1536]{1,0:T(8,128)(2,1)} %shard_map.109) | data formatting | bytes 1572864

commit v5 on v4

--- a/solution.py
+++ b/solution.py
@@ -23,10 +23,11 @@
 BLOCKS = CHIP_ROWS // HALF
 REACH = 3
 CHUNKS = OWN * BLOCKS
-LAG = 3
+Q_AT = (0, 2, 5, 8)
+O_AT = (17, 14, 11, 8)
 SLOTS = 4
 POOLED = ((0, 3), (3, 2), (5, 1))
-SPAN = 2 * REACH * LAG
+SPAN = O_AT[0]
 WIDTH = HEADS * HD
 LEAD = 24
 MROWS = 72
@@ -54,9 +55,9 @@
     q_ref, k_ref, v_ref, x_ref, pf_ref, pc_ref, uf_ref, uc_ref, ng_ref, wq_ref, wo_ref,
     out_ref,
     qx, kx, vx, xx, qbuf, oin, oout, sin, sout, vt, fout, fine, mid, summit, pooled, na, wqs, pt, hb,
-    kb, vb, osc, att, ah, ls, lb, wof,
+    kv, osc, att, ah, ls, lb, wof,
     i_sem, x_send, x_recv, q_send, q_recv, o_send, o_recv, s_send, s_recv, f_send, f_recv, e_send, e_recv, w_send, w_recv,
-    n_send, n_recv, u_send, u_recv, k_send, k_recv, v_send, v_recv, a_send, a_recv, l_send, l_recv, up_send, up_recv, down_send, down_recv,
+    n_send, n_recv, u_send, u_recv, k_send, k_recv, a_send, a_recv, l_send, l_recv, up_send, up_recv, down_send, down_recv,
 ):
     ctx = lax.axis_index("ctx")
     sub = lax.axis_index("sub")
@@ -279,14 +280,14 @@
 
     def guarded(i, steps_q, steps_o):
         for s in steps_q:
-            g = i - s * LAG
+            g = i - Q_AT[s]
 
             @pl.when((g >= 0) & (g < CHUNKS))
             def _(s=s, g=g):
                 forward(s, g)
 
         for s in steps_o:
-            g = i - (2 * REACH - s) * LAG
+            g = i - O_AT[s]
 
             @pl.when((g >= 0) & (g < CHUNKS))
             def _(s=s, g=g):
@@ -309,13 +310,13 @@
 
     def steady(i, carry):
         for s in range(REACH):
-            g = i - s * LAG
+            g = i - Q_AT[s]
 
             @pl.when(g < CHUNKS)
             def _(s=s, g=g):
                 forward(s, g)
 
-        at = {s: i - (2 * REACH - s) * LAG for s in range(REACH + 1)}
+        at = {s: i - O_AT[s] for s in range(REACH + 1)}
         q_copy(REACH - 1, at[REACH]).wait_recv()
         states = {s: partial(s, at[s]) for s in range(REACH, -1, -1)}
         for s in range(REACH, -1, -1):
@@ -337,7 +338,7 @@
     halves(1).wait_recv()
     halves(3).wait_recv()
     lax.fori_loop(REACH, SPAN, ramp_up, 0)
-    lax.fori_loop(SPAN, CHUNKS + REACH * LAG, steady, 0)
+    lax.fori_loop(SPAN, CHUNKS + O_AT[REACH], steady, 0)
 
     def edge_arrival(h, side):
         head = side * OWN + h
@@ -388,7 +389,7 @@
         first, count = POOLED[batch]
         for h in range(first, first + count):
             pool(h)
-        for step in range(1, n_chip):
+        for step in sorted(range(1, n_chip), key=lambda step: abs(step - n_chip // 2)):
             n_copy(batch, step).start()
 
         @pl.when(core == 1)
@@ -401,7 +402,7 @@
 
     share(0)
     pass_on(down, 1)
-    lax.fori_loop(CHUNKS + REACH * LAG, CHUNKS + SPAN - 2, ramp_down, 0)
+    lax.fori_loop(CHUNKS + O_AT[REACH], CHUNKS + SPAN - 2, ramp_down, 0)
     share(1)
     pass_on(down, 2)
     lax.fori_loop(CHUNKS + SPAN - 2, CHUNKS + SPAN, ramp_down, 0)
@@ -412,18 +413,16 @@
         piece = unit // 8
         head = piece % CHEADS
         at = pl.multiple_of((piece // CHEADS) * HD + (unit % 8) * UNIT, UNIT)
+        kind = (piece // CHEADS + 1) // 2
         src, dst = pt.at[pl.ds(i * UNIT, UNIT)], hb.at[pl.ds(at, UNIT)]
         return (
             head,
-            lambda: remote(src, dst, u_send.at[i], u_recv.at[0], (ctx, 2 * head)),
-            lambda: pltpu.make_async_copy(src, dst, u_recv.at[0]),
+            lambda: remote(src, dst, u_send.at[i], u_recv.at[kind], (ctx, 2 * head)),
+            lambda: pltpu.make_async_copy(src, dst, u_recv.at[kind]),
         )
 
     def k_copy(source, step):
-        return remote(kb.at[source], kb.at[source], k_send.at[step], k_recv.at[source], (source + step, sub))
-
-    def v_copy(source, step):
-        return remote(vb.at[source], vb.at[source], v_send.at[step], v_recv.at[source], (source + step, sub))
+        return remote(kv.at[source], kv.at[source], k_send.at[step], k_recv.at[source], (source + step, sub))
 
     def a_copy(step):
         target = (sub + step) % n_sub
@@ -471,14 +470,13 @@
 
     @pl.when((core == 0) & (zc < CHEADS))
     def _():
-        pltpu.make_async_copy(hb, hb, u_recv.at[0]).wait()
-        kb[ctx] = hb[HD : 2 * HD].astype(F32).T.astype(BF16)
-        vb[ctx] = hb[2 * HD : 3 * HD]
+        pair = hb.at[pl.ds(HD, 2 * HD)]
+        pltpu.make_async_copy(pair, pair, u_recv.at[1]).wait()
+        kv[ctx] = hb[HD : 3 * HD]
         for step in range(1, n_ctx):
             @pl.when(ctx + step < n_ctx)
             def _(step=step):
                 k_copy(ctx, step).start()
-                v_copy(ctx, step).start()
 
     for hop in range(4, n_down + 1):
         pass_on(down, hop)
@@ -496,31 +494,36 @@
 
     @pl.when((core == 0) & (zc < CHEADS))
     def _():
+        first = hb.at[pl.ds(0, HD)]
+        pltpu.make_async_copy(first, first, u_recv.at[0]).wait()
         queries = hb[0:HD].astype(F32).T.astype(BF16)
-        t = nt(kb[ctx], queries) * SCALE
+
+        def scored(source):
+            return nt(kv[source, 0:HD].astype(F32).T.astype(BF16), queries) * SCALE
+
+        t = scored(ctx)
         key_row = lax.broadcasted_iota(jnp.int32, t.shape, 0)
         query_row = lax.broadcasted_iota(jnp.int32, t.shape, 1)
         t = jnp.where(key_row <= query_row, t, NEG)
         peak = jnp.max(t, axis=0, keepdims=True)
         p = jnp.exp2(t - peak)
         total = jnp.sum(p, axis=0, keepdims=True)
-        osc[...] = dot(vb[ctx], p.astype(BF16))
+        osc[...] = dot(kv[ctx, HD : 2 * HD], p.astype(BF16))
 
         def fold(i, carry):
             before, total = carry
             source = ctx - 1 - i
             k_copy(source, 1).wait_recv()
-            v_copy(source, 1).wait_recv()
-            t = nt(kb[source], queries) * SCALE
+            t = scored(source)
             peak = jnp.maximum(before, jnp.max(t, axis=0, keepdims=True))
             p = jnp.exp2(t - peak)
             a = jnp.exp2(before - peak)
-            osc[...] = osc[...] * a + dot(vb[source], p.astype(BF16))
+            osc[...] = osc[...] * a + dot(kv[source, HD : 2 * HD], p.astype(BF16))
             return peak, total * a + jnp.sum(p, axis=0, keepdims=True)
 
         peak, total = lax.fori_loop(0, ctx, fold, (peak, total))
         att[...] = (osc[...] / total).T.astype(BF16)
-        for step in range(1, n_sub):
+        for step in sorted(range(1, n_sub), key=lambda step: abs(step - n_sub // 2)):
             a_copy(step).start()
         ah[zc] = att[pl.ds(pl.multiple_of(zc * 2 * UNIT, 2 * UNIT), 2 * UNIT), :]
 
@@ -608,7 +611,6 @@
             @pl.when(ctx + step < n_ctx)
             def _(step=step):
                 k_copy(ctx, step).wait_send()
-                v_copy(ctx, step).wait_send()
         for step in range(1, n_sub):
             a_copy(step).wait_send()
 
@@ -642,8 +644,7 @@
                 pltpu.VMEM((QKV_COLS, WIDTH), BF16),
                 pltpu.VMEM((2 * QKV_COLS, ROWS), BF16),
                 pltpu.VMEM((3 * HD, ROWS), BF16),
-                pltpu.VMEM((n_ctx, ROWS, HD), BF16),
-                pltpu.VMEM((n_ctx, HD, ROWS), BF16),
+                pltpu.VMEM((n_ctx, 2 * HD, ROWS), BF16),
                 pltpu.VMEM((HD, ROWS), F32),
                 pltpu.VMEM((ROWS, HD), BF16),
                 pltpu.VMEM((CHEADS, 2 * UNIT, HD), BF16),
@@ -658,8 +659,7 @@
                 dma((OWN, 2)), dma((OWN, 2)),
                 dma((1,)), dma((1,)),
                 dma((len(POOLED), n_chip)), dma((len(POOLED), n_sub)),
-                dma((18,)), dma((1,)),
-                dma((n_ctx,)), dma((n_ctx,)),
+                dma((18,)), dma((2,)),
                 dma((n_ctx,)), dma((n_ctx,)),
                 dma((n_sub,)), dma((CHEADS,)),
                 dma((1,)), dma((1,)),

time: 140 us -> 140 us (level)
  no operation moved by 1% of the time
where the time goes in v5:
time: 140 us
  Pallas kernels  138 us (99%)
  local copies, waits for them, and re-layouts  2.06 us (1%)
    pallas_call x1, Pallas kernels, shards(): pl.pallas_call(functools.partial(kernel, n_ctx, n_sub), out_shape=jax.Sha...  138 us

profile of v5, /device:TPU:29, one launch (start us, length us, event | category | flops | bytes accessed | tf_op | source)
XLA Modules:
  0.0 139.7 jit_solution(3800064742967729580)
XLA Ops:
  0.0 137.6 %shard_map.109 = bf16[256,1536]{1,0:T(8,128)(2,1)} custom-call(bf16[256,1536]{1,0:T(8,128)(2,1)} %q_ref.1, bf16[256,1536]{1,0:T(8,128)(2,1)} %k_ref.1, bf16[256,1536]{1,0:T(8,128)(2,1)} %v_ref.1, bf16[256,1536]{1,0:T(8,128)(2,1)} %x_ref.1, f32[4,1536]{1,0:T(4,128)} %pf_ref.1, f32[4,1536]{1,0:T(4,128)} %pc_ref.1, f32[4,1536]{1,0:T(4,128)} %uf_ref.1, ...), custom_call_target="tpu_custom_call" | custom-call | tf_op jit(solution)/shard_map/pallas_call | solution.py:625
  137.6 2.1 %copy.13 = bf16[256,1536]{1,0:T(8,128)(2,1)} copy(bf16[256,1536]{1,0:T(8,128)(2,1)} %shard_map.109) | data formatting | bytes 1572864

commit v6 on v5

--- a/solution.py
+++ b/solution.py
@@ -636,7 +636,7 @@
                 pltpu.VMEM((REACH, SLOTS, 2, HALF), F32),
                 pltpu.VMEM((OWN, HD, CHIP_ROWS), BF16),
                 pltpu.VMEM((OWN, 4, HALF, HD), F32),
-                pltpu.VMEM((HEADS, LEAD + ROWS, HD), F32),
+                pltpu.VMEM((HEADS, LEAD + ROWS + 24, HD), F32),
                 pltpu.VMEM((HEADS, MROWS, HD), F32),
                 pltpu.VMEM((16, WIDTH), F32),
                 pltpu.VMEM((OWN, 16, 2 * HD), BF16),

time: 140 us -> 140 us (level)
  no operation moved by 1% of the time
where the time goes in v6:
time: 140 us
  Pallas kernels  138 us (99%)
  local copies, waits for them, and re-layouts  2.06 us (1%)
    pallas_call x1, Pallas kernels, shards(): pl.pallas_call(functools.partial(kernel, n_ctx, n_sub), out_shape=jax.Sha...  138 us

profile of v6, /device:TPU:29, one launch (start us, length us, event | category | flops | bytes accessed | tf_op | source)
XLA Modules:
  0.0 139.7 jit_solution(2024611919918014204)
XLA Ops:
  0.0 137.6 %shard_map.109 = bf16[256,1536]{1,0:T(8,128)(2,1)} custom-call(bf16[256,1536]{1,0:T(8,128)(2,1)} %q_ref.1, bf16[256,1536]{1,0:T(8,128)(2,1)} %k_ref.1, bf16[256,1536]{1,0:T(8,128)(2,1)} %v_ref.1, bf16[256,1536]{1,0:T(8,128)(2,1)} %x_ref.1, f32[4,1536]{1,0:T(4,128)} %pf_ref.1, f32[4,1536]{1,0:T(4,128)} %pc_ref.1, f32[4,1536]{1,0:T(4,128)} %uf_ref.1, ...), custom_call_target="tpu_custom_call" | custom-call | tf_op jit(solution)/shard_map/pallas_call | solution.py:625
  137.6 2.1 %copy.13 = bf16[256,1536]{1,0:T(8,128)(2,1)} copy(bf16[256,1536]{1,0:T(8,128)(2,1)} %shard_map.109) | data formatting | bytes 1572864
